TPU v7x, 32 devices: a whole 2x2x4 slice. The times are simulated.
32 devices in a mesh: dp: 2 (over x), seq: 4 (over z), tensor: 4 (over y, core).
Axes of the slice: x: 2, y: 2, z: 4, core: 2. Of those that a mesh axis runs over, the one named last changes fastest.
Arguments:
- inputs: bfloat16 [2, 2048, 768], P('dp', ('seq', 'tensor')), may hold values from -6 to 6
- ln1_gain: bfloat16 [768], replicated, may hold values from 0.099609375 to 1.8984375
- ln1_bias: bfloat16 [768], replicated, may hold values from -3 to 3
- w_query: bfloat16 [768, 768], P(None, 'tensor'), may hold values from -0.21875 to 0.21875
- b_query: bfloat16 [768], P('tensor'), may hold values from -3 to 3
- w_key: bfloat16 [768, 768], P(None, 'tensor'), may hold values from -0.21875 to 0.21875
- w_value: bfloat16 [768, 768], P(None, 'tensor'), may hold values from -0.21875 to 0.21875
- b_value: bfloat16 [768], P('tensor'), may hold values from -3 to 3
- w_out: bfloat16 [768, 768], P('tensor'), may hold values from -3.5 to 3.5
- b_out: bfloat16 [768], replicated, may hold values from -1.75 to 1.75
- ln2_gain: bfloat16 [768], replicated, may hold values from 0.099609375 to 1.8984375
- ln2_bias: bfloat16 [768], replicated, may hold values from -3 to 3
- w_up: bfloat16 [768, 3072], P(None, 'tensor'), may hold values from -0.21875 to 0.21875
- b_up: bfloat16 [3072], P('tensor'), may hold values from -3 to 3
- w_down: bfloat16 [3072, 768], P('tensor'), may hold values from -0.109375 to 0.109375
- b_down: bfloat16 [768], replicated, may hold values from -1.75 to 1.75
- cotangent: bfloat16 [2, 2048, 768], P('dp', ('seq', 'tensor')), may hold values from -6 to 6
Outputs:
- output: bfloat16 [2, 2048, 768], P('dp', ('seq', 'tensor'))
- input_grad: bfloat16 [2, 2048, 768], P('dp', ('seq', 'tensor'))
- grad_ln1_gain: float32 [768], P('tensor')
- grad_ln1_bias: float32 [768], P('tensor')
- grad_w_query: float32 [768, 768], P(None, 'tensor')
- grad_b_query: float32 [768], P('tensor')
- grad_w_key: float32 [768, 768], P(None, 'tensor')
- grad_w_value: float32 [768, 768], P(None, 'tensor')
- grad_b_value: float32 [768], P('tensor')
- grad_w_out: float32 [768, 768], P('tensor')
- grad_b_out: float32 [768], P('tensor')
- grad_ln2_gain: float32 [768], P('tensor')
- grad_ln2_bias: float32 [768], P('tensor')
- grad_w_up: float32 [768, 3072], P(None, 'tensor')
- grad_b_up: float32 [3072], P('tensor')
- grad_w_down: float32 [3072, 768], P('tensor')
- grad_b_down: float32 [768], P('tensor')
All inputs are finite; a program needn't handle non-finite values.
Results may differ from a plain program's by a relative error of at most 0.01.
The roundings to bfloat16 on the way count: a program that leaves them out, or rounds other values in their place, can miss the bound.
Values may be sent and summed in bfloat16 or wider, within the bound.
A program may use at most 128 MiB of HBM per device.

v0:
```python
from functools import partial

import jax
import jax.numpy as jnp
from jax import lax
from jax.sharding import PartitionSpec as P

HEAD_DIM = 64


eps = 1e-05


def product(left, right):
    return jnp.dot(left, right, preferred_element_type=jnp.float32)


def product_rows(left, right):
    return lax.dot_general(
        left, right, (((0,), (0,)), ((), ())), preferred_element_type=jnp.float32
    )


def product_cols(left, right):
    return lax.dot_general(
        left, right, (((1,), (1,)), ((), ())), preferred_element_type=jnp.float32
    )


def normalize(values, gain, offset):
    center = values - jnp.mean(values, axis=-1, keepdims=True)
    spread = lax.rsqrt(jnp.mean(center * center, axis=-1, keepdims=True) + eps)
    scaled = center * spread
    return (scaled * gain + offset, scaled, spread)


def normalize_back(upstream, scaled, spread, gain):
    inner = upstream * gain
    return spread * (
        inner
        - jnp.mean(inner, axis=-1, keepdims=True)
        - scaled * jnp.mean(inner * scaled, axis=-1, keepdims=True)
    )


def rows_of(array, start, count):
    return lax.dynamic_slice_in_dim(array, start, count, 0)


def local(
    inputs,
    ln1_gain,
    ln1_bias,
    w_query,
    b_query,
    w_key,
    w_value,
    b_value,
    w_out,
    b_out,
    ln2_gain,
    ln2_bias,
    w_up,
    b_up,
    w_down,
    b_down,
    cotangent,
):
    frames_in = inputs[0].astype(jnp.float32)
    own_rows = frames_in.shape[0]
    gain_one = ln1_gain.astype(jnp.float32)
    gain_two = ln2_gain.astype(jnp.float32)
    normed_one, scaled_one, spread_one = normalize(
        frames_in, gain_one, ln1_bias.astype(jnp.float32)
    )
    attn_input = lax.all_gather(normed_one.astype(jnp.bfloat16), "tensor", axis=0, tiled=True)
    query = (product(attn_input, w_query) + b_query.astype(jnp.float32)).astype(jnp.bfloat16)
    keys = product(attn_input, w_key).astype(jnp.bfloat16)
    values = (product(attn_input, w_value) + b_value.astype(jnp.float32)).astype(jnp.bfloat16)
    key_all, value_all = (
        lax.all_gather(keys, "seq", axis=0, tiled=True),
        lax.all_gather(values, "seq", axis=0, tiled=True),
    )
    frames = query.shape[0]
    heads = query.shape[1] // HEAD_DIM
    scale = HEAD_DIM ** (-0.5)
    query3 = query.reshape(frames, heads, HEAD_DIM)
    key3 = key_all.reshape(key_all.shape[0], heads, HEAD_DIM)
    value3 = value_all.reshape(value_all.shape[0], heads, HEAD_DIM)
    scores = jnp.einsum("qhd,khd->hqk", query3, key3, preferred_element_type=jnp.float32) * scale
    top = jnp.max(scores, axis=-1, keepdims=True)
    expo = jnp.exp(scores - top)
    total = jnp.sum(expo, axis=-1, keepdims=True)
    logsum = top + jnp.log(total)
    weights_low = (expo / total).astype(jnp.bfloat16)
    context = jnp.einsum("hqk,khd->qhd", weights_low, value3, preferred_element_type=jnp.float32)
    context = context.reshape(frames, heads * HEAD_DIM).astype(jnp.bfloat16)
    attn_rows = lax.psum_scatter(
        product(rows_of(context, jnp.int32(0), lax.axis_size("tensor") * own_rows), w_out),
        "tensor",
        scatter_dimension=0,
        tiled=True,
    )
    middle = frames_in + attn_rows + b_out.astype(jnp.float32)
    normed_two, scaled_two, spread_two = normalize(middle, gain_two, ln2_bias.astype(jnp.float32))
    mlp_input = lax.all_gather(normed_two.astype(jnp.bfloat16), "tensor", axis=0, tiled=True)
    before = product(mlp_input, w_up) + b_up.astype(jnp.float32)
    activated, gelu_back = jax.vjp(partial(jax.nn.gelu, approximate=False), before)
    hidden = activated.astype(jnp.bfloat16)
    mlp_rows = lax.psum_scatter(
        product(rows_of(hidden, jnp.int32(0), lax.axis_size("tensor") * own_rows), w_down).astype(
            jnp.bfloat16
        ),
        "tensor",
        scatter_dimension=0,
        tiled=True,
    ).astype(jnp.float32)
    result = (middle + mlp_rows + b_down.astype(jnp.float32)).astype(jnp.bfloat16)
    upstream = cotangent[0].astype(jnp.float32)
    grad_z_rows = upstream.astype(jnp.bfloat16)
    grad_z_all = lax.all_gather(grad_z_rows, "tensor", axis=0, tiled=True)
    grad_down = product_rows(hidden, grad_z_all)
    grad_hidden = product_cols(grad_z_all, w_down)
    (grad_before,) = gelu_back(grad_hidden)
    grad_before = grad_before.astype(jnp.bfloat16)
    grad_up = product_rows(mlp_input, grad_before)
    grad_bup = jnp.sum(grad_before.astype(jnp.float32), axis=0)
    mlp_sums = (grad_up, grad_bup, grad_down)
    grad_two = lax.psum_scatter(
        product_cols(rows_of(grad_before, jnp.int32(0), lax.axis_size("tensor") * own_rows), w_up),
        "tensor",
        scatter_dimension=0,
        tiled=True,
    )
    grad_middle = upstream + normalize_back(grad_two, scaled_two, spread_two, gain_two)
    grad_attn_rows = grad_middle.astype(jnp.bfloat16)
    grad_attn_all = lax.all_gather(grad_attn_rows, "tensor", axis=0, tiled=True)
    grad_wout = product_rows(context, grad_attn_all)
    grad_context = (
        product_cols(grad_attn_all, w_out).astype(jnp.bfloat16).reshape(frames, heads, HEAD_DIM)
    )
    scores_again = (
        jnp.einsum("qhd,khd->hqk", query3, key3, preferred_element_type=jnp.float32) * scale
    )
    probs = jnp.exp(scores_again - logsum)
    probs_low = probs.astype(jnp.bfloat16)
    grad_probs = jnp.einsum(
        "qhd,khd->hqk", grad_context, value3, preferred_element_type=jnp.float32
    )
    inner_sum = jnp.sum(probs * grad_probs, axis=-1, keepdims=True)
    grad_scores = (probs * (grad_probs - inner_sum)).astype(jnp.bfloat16)
    grad_query = (
        jnp.einsum("hqk,khd->qhd", grad_scores, key3, preferred_element_type=jnp.float32) * scale
    )
    grad_query = grad_query.reshape(frames, heads * HEAD_DIM).astype(jnp.bfloat16)
    key_terms = (
        jnp.einsum("hqk,qhd->khd", grad_scores, query3, preferred_element_type=jnp.float32) * scale
    )
    key_terms = key_terms.reshape(key_all.shape[0], heads * HEAD_DIM)
    value_terms = jnp.einsum(
        "hqk,qhd->khd", probs_low, grad_context, preferred_element_type=jnp.float32
    )
    value_terms = value_terms.reshape(value_all.shape[0], heads * HEAD_DIM)
    grad_keys, grad_values = (
        lax.psum_scatter(key_terms, "seq", scatter_dimension=0, tiled=True),
        lax.psum_scatter(value_terms, "seq", scatter_dimension=0, tiled=True),
    )
    grad_keys = grad_keys.astype(jnp.bfloat16)
    grad_values = grad_values.astype(jnp.bfloat16)
    grad_wq = product_rows(attn_input, grad_query)
    grad_bq = jnp.sum(grad_query.astype(jnp.float32), axis=0)
    grad_wk = product_rows(attn_input, grad_keys)
    grad_wv = product_rows(attn_input, grad_values)
    grad_bv = jnp.sum(grad_values.astype(jnp.float32), axis=0)
    start = jnp.int32(0)
    term = product_cols(rows_of(grad_query, start, lax.axis_size("tensor") * own_rows), w_query)
    term = term + product_cols(rows_of(grad_keys, start, lax.axis_size("tensor") * own_rows), w_key)
    grad_one = lax.psum_scatter(
        term
        + product_cols(rows_of(grad_values, start, lax.axis_size("tensor") * own_rows), w_value),
        "tensor",
        scatter_dimension=0,
        tiled=True,
    )
    grad_input = (grad_middle + normalize_back(grad_one, scaled_one, spread_one, gain_one)).astype(
        jnp.bfloat16
    )
    stacked = jnp.stack(
        [
            jnp.sum(grad_one * scaled_one, axis=0),
            jnp.sum(grad_one, axis=0),
            jnp.sum(grad_attn_rows.astype(jnp.float32), axis=0),
            jnp.sum(grad_two * scaled_two, axis=0),
            jnp.sum(grad_two, axis=0),
            jnp.sum(grad_z_rows.astype(jnp.float32), axis=0),
        ]
    )
    vector_total = lax.psum(stacked, ("dp", "seq", "tensor"))
    width = vector_total.shape[1] // lax.axis_size("tensor")
    shares = lax.dynamic_slice_in_dim(vector_total, lax.axis_index("tensor") * width, width, 1)
    every = lax.psum(
        (
            grad_wq,
            grad_bq,
            grad_wk,
            grad_wv,
            grad_bv,
            grad_wout,
            mlp_sums[0],
            mlp_sums[1],
            mlp_sums[2],
        ),
        ("dp", "seq"),
    )
    attn_sums = every[:6]
    mlp_sums = every[6:]
    return (
        result[None],
        grad_input[None],
        shares[0],
        shares[1],
        attn_sums[0],
        attn_sums[1],
        attn_sums[2],
        attn_sums[3],
        attn_sums[4],
        attn_sums[5],
        shares[2],
        shares[3],
        shares[4],
        mlp_sums[0],
        mlp_sums[1],
        mlp_sums[2],
        shares[5],
    )


def solution(mesh):
    placed = (
        P("dp", ("seq", "tensor"), None),
        P(),
        P(),
        P(None, "tensor"),
        P("tensor"),
        P(None, "tensor"),
        P(None, "tensor"),
        P("tensor"),
        P("tensor", None),
        P(),
        P(),
        P(),
        P(None, "tensor"),
        P("tensor"),
        P("tensor", None),
        P(),
        P("dp", ("seq", "tensor"), None),
    )
    return jax.shard_map(
        local,
        mesh=mesh,
        in_specs=placed,
        out_specs=(
            P("dp", ("seq", "tensor"), None),
            P("dp", ("seq", "tensor"), None),
            P("tensor"),
            P("tensor"),
            P(None, "tensor"),
            P("tensor"),
            P(None, "tensor"),
            P(None, "tensor"),
            P("tensor"),
            P("tensor", None),
            P("tensor"),
            P("tensor"),
            P("tensor"),
            P(None, "tensor"),
            P("tensor"),
            P("tensor", None),
            P("tensor"),
        ),
        check_vma=False,
    )
```

profile of v0, /device:TPU:0, one launch (start us, length us, event | category | flops | bytes accessed | tf_op | source)
XLA Modules:
  0.0 570.9 jit_solution(1523307849775323217)
XLA Ops:
  7.3 0.8 convert_element_type.129
  8.1 0.7 convert_element_type.128
  8.7 1.0 convert_reduce_fusion.2
  9.8 1.1 fusion.39
  11.5 1.1 fusion.32
  12.6 10.2 %all_gather.18 = bf16[512,768]{1,0:T(8,128)(2,1)S(1)} all-gather(bf16[128,768]{1,0:T(8,128)(2,1)S(1)} %fusion.32), channel_id=1, replica_groups=mesh['dp'=2,'seq'=4,'tensor'=4] {'tensor'}, dimensions={0}, use_global_device_ids=true | all-gather | bytes 983040 | tf_op jit(solution)/shard_map/all_gather | solution.py:76
  23.3 19.9 %all_gather.19 = bf16[2048,192]{0,1:T(8,128)(2,1)S(1)} all-gather(bf16[512,192]{0,1:T(8,128)(2,1)S(1)} %fusion.13), channel_id=1, replica_groups=mesh['dp'=2,'seq'=4,'tensor'=4] {'seq'}, dimensions={0}, use_global_device_ids=true | all-gather | bytes 983040 | tf_op jit(solution)/shard_map/all_gather | solution.py:82
  43.6 18.2 %all_gather.20 = bf16[2048,192]{0,1:T(8,128)(2,1)S(1)} all-gather(bf16[512,192]{0,1:T(8,128)(2,1)S(1)} %convolution_convert_fusion.2), channel_id=1, replica_groups=mesh['dp'=2,'seq'=4,'tensor'=4] {'seq'}, dimensions={0}, use_global_device_ids=true | all-gather | bytes 983040 | tf_op jit(solution)/shard_map/all_gather | solution.py:81
  62.2 1.9 multiply_reduce_fusion.1
  64.2 2.5 fusion
  66.7 2.0 copy-done.2
  68.7 3.4 fusion.16
  72.1 0.7 copy-done.23
  72.8 1.6 fusion.58
  74.5 0.6 convert_element_type.144
  75.1 0.6 convert_element_type.140
  75.7 8.6 %all-gather = bf16[1,512,768]{2,1,0:T(8,128)(2,1)} all-gather(bf16[1,128,768]{2,1,0:T(8,128)(2,1)S(1)} %copy-done.14), channel_id=2, replica_groups=mesh['dp'=2,'seq'=4,'tensor'=4] {'tensor'}, dimensions={1}, use_global_device_ids=true | all-gather | bytes 983040 | tf_op jit(solution)/shard_map/all_gather | solution.py:121
  84.3 17.4 %reduce-scatter.7.cloned.1.call-done = f32[128,768]{1,0:T(8,128)} async-done(((f32[512,768]{1,0:T(8,128)}), f32[128,768]{1,0:T(8,128)}) %reduce-scatter.7.cloned.1.call-update) | async-done | bytes 393232 | tf_op jit(solution)/shard_map/reduce_scatter | solution.py:98
  101.8 1.2 fusion.55
  103.7 8.2 %all_gather.21 = bf16[512,768]{1,0:T(8,128)(2,1)S(1)} all-gather(bf16[128,768]{1,0:T(8,128)(2,1)S(1)} %add_convert_fusion.2), channel_id=1, replica_groups=mesh['dp'=2,'seq'=4,'tensor'=4] {'tensor'}, dimensions={0}, use_global_device_ids=true | all-gather | bytes 983040 | tf_op jit(solution)/shard_map/all_gather | solution.py:106
  111.9 5.2 multiply_convert_fusion.1
  117.2 1.8 convert_reduce_fusion
  118.9 0.9 copy-done.22
  119.8 2.0 fusion.59
  121.9 1.1 copy-done.12
  122.9 3.0 convolution_convert_fusion
  126.0 24.5 %reduce-scatter.11.cloned.1.call-done = f32[128,768]{1,0:T(8,128)} async-done(((f32[512,768]{1,0:T(8,128)}), f32[128,768]{1,0:T(8,128)}) %reduce-scatter.11.cloned.1.call-update) | async-done | bytes 393232 | tf_op jit(solution)/shard_map/reduce_scatter | solution.py:129
  150.6 1.2 multiply_reduce_fusion.2
  151.8 25.2 %reduce-scatter.9.cloned.1.call-done = bf16[128,768]{1,0:T(8,128)(2,1)} async-done(((bf16[512,768]{1,0:T(8,128)(2,1)}), bf16[128,768]{1,0:T(8,128)(2,1)}) %reduce-scatter.9.cloned.1.call-update) | async-done | bytes 196624 | tf_op jit(solution)/shard_map/reduce_scatter | solution.py:110
  177.0 2.7 convert_reduce_fusion.5
  179.6 8.4 %all_gather.23 = bf16[512,768]{1,0:T(8,128)(2,1)S(1)} all-gather(bf16[128,768]{1,0:T(8,128)(2,1)S(1)} %get-tuple-element.35), channel_id=1, replica_groups=mesh['dp'=2,'seq'=4,'tensor'=4] {'tensor'}, dimensions={0}, use_global_device_ids=true | all-gather | bytes 983040 | tf_op jit(solution)/shard_map/all_gather | solution.py:137
  188.0 1.4 convolution_convert_fusion.1
  189.4 6.9 %multiply_reduce_fusion = (f32[3,512]{1,0:T(4,128)S(1)}, f32[3,512,2048]{2,1,0:T(8,128)S(1)}) fusion(f32[3,512,2048]{2,1,0:T(8,128)} %copy-done.2, f32[3,512]{1,0:T(4,128)S(1)} %log_add_fusion, bf16[512,3,64]{0,2,1:T(8,128)(2,1)S(1)} %bitcast.129, bf16[2048,3,64]{0,2,1:T(8,128)(2,1)} %bitcast.128), kind=kOutput, calls=%fused_computation.1 | convolution fusion | flops 415234560 | bytes 26161152 | tf_op jit(solution)/shard_map/qhd,khd->hqk/dot_general | solution.py:147
  196.7 1.2 slice-done.2
  197.9 4.7 multiply_convert_fusion
  202.5 5.1 convolution_multiply_fusion
  207.7 8.1 %fusion.2 = f32[3,64,2048]{2,1,0:T(8,128)} fusion(bf16[512,3,64]{0,2,1:T(8,128)(2,1)S(1)} %bitcast.130, f32[3,512,2048]{2,1,0:T(8,128)} %copy-done.2, f32[3,512]{1,0:T(4,128)S(1)} %log_add_fusion), kind=kOutput, calls=%fused_computation.8 | convolution fusion | flops 412090368 | bytes 14358528 | tf_op jit(solution)/shard_map/hqk,qhd->khd/dot_general | solution.py:160
  215.9 4.9 convert_reduce_fusion.4
  220.8 1.6 fusion.60
  222.4 21.2 %reduce-scatter.13.cloned.1.call-done = f32[512,192]{0,1:T(8,128)} async-done(((f32[2048,192]{0,1:T(8,128)}), f32[512,192]{0,1:T(8,128)}) %reduce-scatter.13.cloned.1.call-update) | async-done | bytes 393232 | tf_op jit(solution)/shard_map/reduce_scatter | solution.py:165
  243.5 2.5 fusion.46
  246.1 34.0 %reduce-scatter.15.cloned.1.call-done = f32[512,192]{0,1:T(8,128)} async-done(((f32[2048,192]{0,1:T(8,128)}), f32[512,192]{0,1:T(8,128)}) %reduce-scatter.15.cloned.1.call-update) | async-done | bytes 393232 | tf_op jit(solution)/shard_map/reduce_scatter | solution.py:166
  280.1 3.6 add_add_fusion
  283.8 1.1 copy-done.5
  284.8 3.5 fusion.62
  288.3 2.2 fusion.17
  290.5 1.1 fusion.63
  291.7 1.1 fusion.61
  292.8 1.1 fusion.44
  293.9 1.1 fusion.48
  295.2 0.5 copy-done.38
  296.0 20.4 %all-reduce = (f32[192]{0:T(256)}, f32[192]{0:T(256)}, f32[768]{0:T(1024)}) all-reduce(f32[192]{0:T(256)S(1)} %reduce_sum.190, f32[192]{0:T(256)S(1)} %convert_reduce_fusion.3, f32[768]{0:T(1024)S(1)} %copy-done.47), channel_id=1, replica_groups=mesh['dp'=2,'seq'=4,'tensor'=4] {'dp','seq'}, use_global_device_ids=true, to_apply=%region_26.0 | all-reduce | flops 1152 | bytes 9216 | tf_op jit(solution)/shard_map/psum | solution.py:201
  316.4 1.2 fusion.38
  317.7 41.6 %psum.70 = f32[6,768]{1,0:T(8,128)S(1)} all-reduce(f32[6,768]{1,0:T(8,128)S(1)} %stack.27), channel_id=1, replica_groups=mesh['dp'=2,'seq'=4,'tensor'=4] {'dp','seq','tensor'}, use_global_device_ids=true, to_apply=%region_23.0 | all-reduce | flops 4608 | bytes 36864 | tf_op jit(solution)/shard_map/psum | solution.py:198
  359.3 0.7 fusion.57
  360.0 1.9 fusion.43
  361.9 193.8 %all-reduce.4.cloned.1.call-done = (f32[768,192]{0,1:T(8,128)}, f32[768,192]{0,1:T(8,128)}, f32[768,192]{0,1:T(8,128)}, f32[192,768]{1,0:T(8,128)}, f32[768,768]{1,0:T(8,128)}, /*index=5*/f32[768,768]{1,0:T(8,128)}) async-done(((f32[768,192]{0,1:T(8,128)}, f32[768,192]{0,1:T(8,128)}, f32[768,192]{0,1:T(8,128)}, f32[192,768]{1,0:T(8,128)}, f32[768,768]{1,0:T(8,128)}, /*index=5*/f32[768,768]{1,0:T(8,128)}), ...) | async-done | bytes 7077904 | tf_op jit(solution)/shard_map/psum | solution.py:201
  555.6 2.0 copy.40
  557.7 0.8 copy.41
  558.5 0.8 copy.42
  559.3 0.8 copy.43
  560.2 1.4 copy.44
  561.6 1.1 copy-done.10
  562.7 1.4 copy.45
  (156 shorter events, 3.8 us)
Async XLA Ops:
  7.2 104.7 %copy-start = (bf16[768,768]{1,0:T(8,128)(2,1)S(1)}, bf16[768,768]{1,0:T(8,128)(2,1)}, u32[]{:S(2)}) copy-start(bf16[768,768]{1,0:T(8,128)(2,1)} %param.29) | copy-start | bytes 3538948
  7.2 15.6 %copy-start.55 = (bf16[192]{0:T(256)(128)(2,1)S(1)}, bf16[192]{0:T(256)(128)(2,1)}, u32[]{:S(2)}) copy-start(bf16[192]{0:T(256)(128)(2,1)} %param.24) | copy-start | bytes 1156
  7.2 15.6 %copy-start.30 = (bf16[768,192]{0,1:T(8,128)(2,1)S(1)}, bf16[768,192]{0,1:T(8,128)(2,1)}, u32[]{:S(2)}) copy-start(bf16[768,192]{0,1:T(8,128)(2,1)} %param.23) | copy-start | bytes 884740
  7.2 94.5 %reduce-scatter.7.cloned.1.call-start = ((), (), s32[]{:S(2)}) async-start(), calls=%async_computation.6 | async-start | bytes 1966080 | tf_op jit(solution)/shard_map/reduce_scatter | solution.py:98
  8.7 2.2 copy-start.32
  9.8 1.2 copy-start.39
  12.6 30.6 %copy-start.56 = (bf16[192]{0:T(256)(128)(2,1)S(1)}, bf16[192]{0:T(256)(128)(2,1)}, u32[]{:S(2)}) copy-start(bf16[192]{0:T(256)(128)(2,1)} %param.21) | copy-start | bytes 1156
  12.6 30.6 %copy-start.17 = (bf16[768,192]{0,1:T(8,128)(2,1)S(1)}, bf16[768,192]{0,1:T(8,128)(2,1)}, u32[]{:S(2)}) copy-start(bf16[768,192]{0,1:T(8,128)(2,1)} %param.22) | copy-start | bytes 884740
  23.2 38.6 %copy-start.28 = (bf16[768,192]{0,1:T(8,128)(2,1)S(1)}, bf16[768,192]{0,1:T(8,128)(2,1)}, u32[]{:S(2)}) copy-start(bf16[768,192]{0,1:T(8,128)(2,1)} %param.20) | copy-start | bytes 884740
  43.2 23.5 %copy-start.6 = (bf16[2048,192]{0,1:T(8,128)(2,1)}, bf16[2048,192]{0,1:T(8,128)(2,1)S(1)}, u32[]{:S(2)}) copy-start(bf16[2048,192]{0,1:T(8,128)(2,1)S(1)} %all_gather.19) | copy-start | bytes 2359300
  62.2 1.9 copy-start.20
  64.2 4.5 copy-start.2
  66.6 5.4 copy-start.36
  68.7 4.1 copy-start.19
  72.1 0.7 copy-start.23
  72.8 1.7 copy-start.49
  72.8 2.3 copy-start.50
  72.8 2.9 copy-start.51
  72.8 2.9 copy-start.52
  72.8 2.9 copy-start.14
  74.4 27.4 %copy-start.3 = (bf16[1,128,768]{2,1,0:T(8,128)(2,1)S(1)}, bf16[1,128,768]{2,1,0:T(8,128)(2,1)}, u32[]{:S(2)}) copy-start(bf16[1,128,768]{2,1,0:T(8,128)(2,1)} %param.17) | copy-start | bytes 589828
  74.4 76.2 %reduce-scatter.11.cloned.1.call-start = ((), (), s32[]{:S(2)}) async-start(), calls=%async_computation.8 | async-start | bytes 1966080 | tf_op jit(solution)/shard_map/reduce_scatter | solution.py:129
  75.7 36.2 %copy-start.34 = (f32[768]{0:T(1024)}, f32[768]{0:T(1024)S(1)}, u32[]{:S(2)}) copy-start(f32[768]{0:T(1024)S(1)} %convert_element_type.141) | copy-start | bytes 9220
  101.8 10.1 %copy-start.48 = (f32[768]{0:T(1024)S(1)}, f32[768]{0:T(1024)}, u32[]{:S(2)}) copy-start(f32[768]{0:T(1024)} %convert_element_type.144) | copy-start | bytes 9220
  111.9 5.3 copy-start.4
  111.9 5.3 copy-start.8
  111.9 5.3 copy-start.54
  118.9 0.9 copy-start.22
  121.8 1.1 copy-start.12
  121.8 55.1 %reduce-scatter.9.cloned.1.call-start = ((), (), s32[]{:S(2)}) async-start(), calls=%async_computation.7 | async-start | bytes 983040 | tf_op jit(solution)/shard_map/reduce_scatter | solution.py:110
  122.9 3.1 copy-start.53
  122.9 3.1 copy-start.37
  122.9 27.6 %copy-start.35 = (f32[768]{0:T(1024)S(1)}, f32[768]{0:T(1024)}, u32[]{:S(2)}) copy-start(f32[768]{0:T(1024)} %copy-done.34) | copy-start | bytes 9220
  122.9 27.6 %copy-start.42 = (f32[128]{0:T(128)S(1)}, f32[128]{0:T(128)}, u32[]{:S(2)}) copy-start(f32[128]{0:T(128)} %copy-done.41) | copy-start | bytes 1540
  122.9 27.6 %copy-start.46 = (f32[128]{0:T(128)S(1)}, f32[128]{0:T(128)}, u32[]{:S(2)}) copy-start(f32[128]{0:T(128)} %copy-done.45) | copy-start | bytes 1540
  125.9 117.6 %reduce-scatter.13.cloned.1.call-start = ((), (), s32[]{:S(2)}) async-start(), calls=%async_computation.9 | async-start | bytes 1966080 | tf_op jit(solution)/shard_map/reduce_scatter | solution.py:165
  189.4 6.9 %slice-start = ((s8[12582912]{0:T(1024)(128)(4,1)}), s8[4194304]{0:T(1024)(128)(4,1)S(1)}, s32[]{:S(2)}) async-start(s8[12582912]{0:T(1024)(128)(4,1)} %bitcast.121), calls=%async_computation.13 | async-start | bytes 8388608
  189.4 7.3 %slice-start.1 = ((s8[12582912]{0:T(1024)(128)(4,1)}), s8[4194304]{0:T(1024)(128)(4,1)S(1)}, s32[]{:S(2)}) async-start(s8[12582912]{0:T(1024)(128)(4,1)} %bitcast.121), calls=%async_computation.14 | async-start | bytes 8388608
  189.4 8.5 %slice-start.2 = ((s8[12582912]{0:T(1024)(128)(4,1)}), s8[4194304]{0:T(1024)(128)(4,1)S(1)}, s32[]{:S(2)}) async-start(s8[12582912]{0:T(1024)(128)(4,1)} %bitcast.121), calls=%async_computation.15 | async-start | bytes 8388608
  197.9 4.7 copy-start.21
  207.7 72.4 %reduce-scatter.15.cloned.1.call-start = ((), (), s32[]{:S(2)}) async-start(), calls=%async_computation.10 | async-start | bytes 1966080 | tf_op jit(solution)/shard_map/reduce_scatter | solution.py:166
  215.8 5.0 copy-start.29
  215.8 100.6 %reduce-scatter.17.cloned.1.call-start = ((), (), s32[]{:S(2)}) async-start(), calls=%async_computation.11 | async-start | bytes 1966080 | tf_op jit(solution)/shard_map/reduce_scatter | solution.py:178
  220.8 22.7 %copy-start.18 = (bf16[768,192]{0,1:T(8,128)(2,1)S(1)}, bf16[768,192]{0,1:T(8,128)(2,1)}, u32[]{:S(2)}) copy-start(bf16[768,192]{0,1:T(8,128)(2,1)} %param.22) | copy-start | bytes 884740
  222.4 57.7 %copy-start.31 = (bf16[768,192]{0,1:T(8,128)(2,1)S(1)}, bf16[768,192]{0,1:T(8,128)(2,1)}, u32[]{:S(2)}) copy-start(bf16[768,192]{0,1:T(8,128)(2,1)} %param.23) | copy-start | bytes 884740
  283.7 1.1 copy-start.5
  283.7 271.9 %all-reduce.4.cloned.1.call-start = ((), (), s32[]{:S(2)}) async-start(), calls=%async_computation.12 | async-start | bytes 14155776 | tf_op jit(solution)/shard_map/psum | solution.py:201
  284.8 3.5 copy-start.9
  284.8 3.5 copy-start.13
  290.5 1.1 copy-start.24
  290.5 2.3 copy-start.16
  291.7 2.3 copy-start.7
  295.1 0.7 copy-start.38
  295.1 0.9 copy-start.47
  295.1 21.3 %copy-start.33 = (f32[768]{0:T(1024)S(1)}, f32[768]{0:T(1024)}, u32[]{:S(2)}) copy-start(f32[768]{0:T(1024)} %copy-done.32) | copy-start | bytes 9220
  295.1 21.3 %copy-start.40 = (f32[128]{0:T(128)S(1)}, f32[128]{0:T(128)}, u32[]{:S(2)}) copy-start(f32[128]{0:T(128)} %copy-done.39) | copy-start | bytes 1540
  295.1 21.3 %copy-start.44 = (f32[128]{0:T(128)S(1)}, f32[128]{0:T(128)}, u32[]{:S(2)}) copy-start(f32[128]{0:T(128)} %copy-done.43) | copy-start | bytes 1540
  295.1 64.8 %copy-start.15 = (f32[128,768]{1,0:T(8,128)S(1)}, f32[128,768]{1,0:T(8,128)}, u32[]{:S(2)}) copy-start(f32[128,768]{1,0:T(8,128)} %get-tuple-element.36) | copy-start | bytes 1179652
  555.6 2.1 copy-start.27
  555.6 2.9 copy-start.26
  555.6 3.7 copy-start.25
  557.7 2.5 copy-start.11
  560.1 2.5 copy-start.10
  560.2 3.9 copy-start.1
  (3 other events, 1.5 us)
Sparse Core Ops, SparseCore 0:
  74.5 27.2 reduce-scatter.6
  121.9 28.5 reduce-scatter.10
  153.7 23.2 reduce-scatter.8
  207.8 35.6 reduce-scatter.12
  245.8 34.2 reduce-scatter.14
  283.8 27.1 reduce-scatter.16
  317.2 238.3 all-reduce.3
where the time goes:
time: 572 us; the launch traced here: 571 us
  waiting for transfers between devices  316 us (55%)
  blocking collectives  136 us (24%)
  matrix products  64.3 us (11%)
  other arithmetic  21.8 us (4%)
  local copies, waits for them, and re-layouts  18.2 us (3%)
  between operations  14.7 us (3%)
    psum x1, waiting for transfers between devices, local(): lax.psum((grad_wq, grad_bq, grad_wk, grad_wv, grad_bv, grad_wout, mlp_sum...  194 us
    psum x1, blocking collectives, local(): vector_total = lax.psum(stacked, ('dp', 'seq', 'tensor'))  41.6 us
    reduce_scatter x1, waiting for transfers between devices, local(): lax.psum_scatter(value_terms, 'seq', scatter_dimension=0, tiled=True)  34 us
    reduce_scatter x1, waiting for transfers between devices, local(): lax.psum_scatter(product(rows_of(hidden, jnp.int32(0), lax.axis_size('ten...  25.2 us
    reduce_scatter x1, waiting for transfers between devices, local(): lax.psum_scatter(product_cols(rows_of(grad_before, jnp.int32(0), lax.axis...  24.5 us
    reduce_scatter x1, waiting for transfers between devices, local(): lax.psum_scatter(key_terms, 'seq', scatter_dimension=0, tiled=True)  21.2 us
    psum x1, blocking collectives, local(): lax.psum((grad_wq, grad_bq, grad_wk, grad_wv, grad_bv, grad_wout, mlp_sum...  20.4 us
    all_gather x1, blocking collectives, local(): lax.all_gather(values, 'seq', axis=0, tiled=True)  19.9 us
  transfers between devices with their start and end apart: 7, of which 6 were waited for; matrix products, arithmetic and copies ran while one was open for 6% of the time, Pallas kernels for 0%

commit v1 on v0

v1 whole, which is shorter than its diff:
```python
from functools import partial

import jax
import jax.numpy as jnp
import numpy as np
from jax import lax
from jax.sharding import PartitionSpec as P

HEAD_DIM = 64


eps = 1e-05


def product(left, right):
    return jnp.dot(left, right, preferred_element_type=jnp.float32)


def product_rows(left, right):
    return lax.dot_general(
        left, right, (((0,), (0,)), ((), ())), preferred_element_type=jnp.float32
    )


def product_cols(left, right):
    return lax.dot_general(
        left, right, (((1,), (1,)), ((), ())), preferred_element_type=jnp.float32
    )


def normalize(values, gain, offset):
    center = values - jnp.mean(values, axis=-1, keepdims=True)
    spread = lax.rsqrt(jnp.mean(center * center, axis=-1, keepdims=True) + eps)
    scaled = center * spread
    return (scaled * gain + offset, scaled, spread)


def normalize_back(upstream, scaled, spread, gain):
    inner = upstream * gain
    return spread * (
        inner
        - jnp.mean(inner, axis=-1, keepdims=True)
        - scaled * jnp.mean(inner * scaled, axis=-1, keepdims=True)
    )


def own_columns(vector, rank, share):
    return lax.dynamic_slice_in_dim(vector, rank * share, share, 0)


def scatter(terms):
    return lax.psum_scatter(
        terms.astype(jnp.bfloat16), "tensor", scatter_dimension=0, tiled=True
    )


def local(
    inputs,
    ln1_gain,
    ln1_bias,
    w_query,
    b_query,
    w_key,
    w_value,
    b_value,
    w_out,
    b_out,
    ln2_gain,
    ln2_bias,
    w_up,
    b_up,
    w_down,
    b_down,
    cotangent,
):
    f32, bf16 = jnp.float32, jnp.bfloat16
    own_rows, width = inputs.shape[1:]
    lanes = lax.axis_size("tensor")
    rank = lax.axis_index("tensor")
    share = width // lanes
    gain_one = ln1_gain.astype(f32)
    gain_two = ln2_gain.astype(f32)
    frames_in = inputs[0].astype(f32)
    both = lax.all_gather(
        jnp.concatenate([inputs[0], cotangent[0]], axis=1), "tensor", axis=0, tiled=True
    )
    grad_z_all = both[:, width:]
    normed_one, scaled_all, _ = normalize(
        both[:, :width].astype(f32), gain_one, ln1_bias.astype(f32)
    )
    attn_input = normed_one.astype(bf16)
    heads_width = w_query.shape[1]
    keys = product(attn_input, w_key).astype(bf16)
    values = (product(attn_input, w_value) + b_value.astype(f32)).astype(bf16)
    kv_all = lax.all_gather(jnp.concatenate([keys, values], axis=1), "seq", axis=0, tiled=True)
    query = (product(attn_input, w_query) + b_query.astype(f32)).astype(bf16)
    grad_hidden = product_cols(grad_z_all, w_down)
    frames = query.shape[0]
    heads = heads_width // HEAD_DIM
    scale = HEAD_DIM ** (-0.5)
    query3 = query.reshape(frames, heads, HEAD_DIM)
    key3 = kv_all[:, :heads_width].reshape(kv_all.shape[0], heads, HEAD_DIM)
    value3 = kv_all[:, heads_width:].reshape(kv_all.shape[0], heads, HEAD_DIM)
    scores = jnp.einsum("qhd,khd->hqk", query3, key3, preferred_element_type=f32) * scale
    top = jnp.max(scores, axis=-1, keepdims=True)
    expo = jnp.exp(scores - top)
    total = jnp.sum(expo, axis=-1, keepdims=True)
    logsum = top + jnp.log(total)
    weights_low = (expo / total).astype(bf16)
    context = jnp.einsum("hqk,khd->qhd", weights_low, value3, preferred_element_type=f32)
    context = context.reshape(frames, heads_width).astype(bf16)
    attn_rows = scatter(product(context, w_out)).astype(f32)
    middle = frames_in + attn_rows + b_out.astype(f32)
    normed_two, scaled_two, spread_two = normalize(middle, gain_two, ln2_bias.astype(f32))
    mlp_input = lax.all_gather(normed_two.astype(bf16), "tensor", axis=0, tiled=True)
    before = product(mlp_input, w_up) + b_up.astype(f32)
    activated, gelu_back = jax.vjp(partial(jax.nn.gelu, approximate=False), before)
    hidden = activated.astype(bf16)
    (grad_before,) = gelu_back(grad_hidden)
    grad_before = grad_before.astype(bf16)
    grad_two = scatter(product_cols(grad_before, w_up)).astype(f32)
    upstream = cotangent[0].astype(f32)
    grad_middle = upstream + normalize_back(grad_two, scaled_two, spread_two, gain_two)
    grad_attn_rows = grad_middle.astype(bf16)
    sums_two = jnp.stack([jnp.sum(grad_two * scaled_two, axis=0), jnp.sum(grad_two, axis=0)])
    high = sums_two.astype(bf16)
    low = (sums_two - high.astype(f32)).astype(bf16)
    extra = jnp.concatenate([high, low, jnp.zeros((12, width), bf16)])
    packed = lax.all_gather(jnp.concatenate([grad_attn_rows, extra]), "tensor", axis=0)
    grad_attn_all = packed[:, :own_rows].reshape(frames, width)
    pair = packed[:, own_rows : own_rows + 4].astype(f32).sum(axis=0)
    pair = lax.dynamic_slice_in_dim(pair[:2] + pair[2:], rank * share, share, 1)
    mlp_rows = scatter(product(hidden, w_down)).astype(f32)
    result = (middle + mlp_rows + b_down.astype(f32)).astype(bf16)
    grad_down = product_rows(hidden, grad_z_all)
    grad_up = product_rows(mlp_input, grad_before)
    grad_wout = product_rows(context, grad_attn_all)
    early = lax.psum(
        (grad_up.astype(bf16), grad_down.astype(bf16), grad_wout.astype(bf16)), ("dp", "seq")
    )
    grad_context = (
        product_cols(grad_attn_all, w_out).astype(bf16).reshape(frames, heads, HEAD_DIM)
    )
    scores_again = jnp.einsum("qhd,khd->hqk", query3, key3, preferred_element_type=f32) * scale
    probs = jnp.exp(scores_again - logsum)
    probs_low = probs.astype(bf16)
    grad_probs = jnp.einsum("qhd,khd->hqk", grad_context, value3, preferred_element_type=f32)
    inner_sum = jnp.sum(probs * grad_probs, axis=-1, keepdims=True)
    grad_scores = (probs * (grad_probs - inner_sum)).astype(bf16)
    key_terms = jnp.einsum("hqk,qhd->khd", grad_scores, query3, preferred_element_type=f32) * scale
    key_terms = key_terms.reshape(kv_all.shape[0], heads_width)
    value_terms = jnp.einsum("hqk,qhd->khd", probs_low, grad_context, preferred_element_type=f32)
    value_terms = value_terms.reshape(kv_all.shape[0], heads_width)
    grad_kv = lax.psum_scatter(
        jnp.concatenate([key_terms, value_terms], axis=1).astype(bf16),
        "seq",
        scatter_dimension=0,
        tiled=True,
    )
    grad_query = jnp.einsum("hqk,khd->qhd", grad_scores, key3, preferred_element_type=f32) * scale
    grad_query = grad_query.reshape(frames, heads_width).astype(bf16)
    grad_keys = grad_kv[:, :heads_width]
    grad_values = grad_kv[:, heads_width:]
    term = (
        product_cols(grad_query, w_query)
        + product_cols(grad_keys, w_key)
        + product_cols(grad_values, w_value)
    )
    grad_one = scatter(term).astype(f32)
    grad_qkv = product_rows(attn_input, jnp.concatenate([grad_query, grad_kv], axis=1))
    grad_qkv, early = lax.optimization_barrier((grad_qkv.astype(bf16), early))
    late = lax.psum(grad_qkv, ("dp", "seq")).astype(f32)
    scaled_one, spread_one = normalize(frames_in, gain_one, ln1_bias.astype(f32))[1:]
    grad_input = (grad_middle + normalize_back(grad_one, scaled_one, spread_one, gain_one)).astype(
        bf16
    )
    sums_one = jnp.concatenate([jnp.sum(term * scaled_all, axis=0), jnp.sum(term, axis=0)])
    sums_one = lax.all_gather(sums_one.reshape(-1, share), "tensor", axis=0)
    sums_one = sums_one.sum(axis=0).reshape(2, lanes, share)
    sums_one = lax.dynamic_index_in_dim(sums_one, rank, 1, keepdims=False)
    mine = [
        sums_one[0],
        sums_one[1],
        jnp.sum(grad_query.astype(f32), axis=0),
        jnp.sum(grad_values.astype(f32), axis=0),
        own_columns(jnp.sum(grad_attn_all.astype(f32), axis=0), rank, share),
        pair[0],
        pair[1],
        own_columns(jnp.sum(grad_z_all.astype(f32), axis=0), rank, share),
        jnp.sum(grad_before.astype(f32), axis=0),
    ]
    ends = np.cumsum([part.shape[0] for part in mine])[:-1]
    totals = lax.all_gather(jnp.concatenate(mine)[None], ("dp", "seq"), axis=0).sum(axis=(0, 1))
    gain1, bias1, bq, bv, bo, gain2, bias2, bd, bu = jnp.split(totals, ends)
    return (
        result[None],
        grad_input[None],
        gain1,
        bias1,
        late[:, :heads_width],
        bq,
        late[:, heads_width : 2 * heads_width],
        late[:, 2 * heads_width :],
        bv,
        early[2].astype(f32),
        bo,
        gain2,
        bias2,
        early[0].astype(f32),
        bu,
        early[1].astype(f32),
        bd,
    )


def solution(mesh):
    placed = (
        P("dp", ("seq", "tensor"), None),
        P(),
        P(),
        P(None, "tensor"),
        P("tensor"),
        P(None, "tensor"),
        P(None, "tensor"),
        P("tensor"),
        P("tensor", None),
        P(),
        P(),
        P(),
        P(None, "tensor"),
        P("tensor"),
        P("tensor", None),
        P(),
        P("dp", ("seq", "tensor"), None),
    )
    return jax.shard_map(
        local,
        mesh=mesh,
        in_specs=placed,
        out_specs=(
            P("dp", ("seq", "tensor"), None),
            P("dp", ("seq", "tensor"), None),
            P("tensor"),
            P("tensor"),
            P(None, "tensor"),
            P("tensor"),
            P(None, "tensor"),
            P(None, "tensor"),
            P("tensor"),
            P("tensor", None),
            P("tensor"),
            P("tensor"),
            P("tensor"),
            P(None, "tensor"),
            P("tensor"),
            P("tensor", None),
            P("tensor"),
        ),
        check_vma=False,
    )
```

time: 572 us -> 490 us (0.86)
  blocking collectives: 136 us -> 52.8 us
  other arithmetic: 21.8 us -> 31 us
  matrix products: 64.3 us -> 55.6 us
  waiting for transfers between devices: 316 us -> 322 us
    psum x2 -> x0, blocking collectives: 62 us -> none  [the longest x1 41.6 us: local(): vector_total = lax.psum(stacked, ('dp', 'seq', 'tensor'))]
    all_gather x0 -> x2, waiting for transfers between devices: none -> 56.9 us  [the longest x1 35.6 us: local(): lax.all_gather(jnp.concatenate([keys, values], axis=1), 'seq', axis=0, ti...]
    psum x1 -> x2, waiting for transfers between devices: 194 us -> 151 us  [the longest x1 118 us: local(): lax.psum((grad_up.astype(bf16), grad_down.astype(bf16), grad_wout.astype(...]
    all_gather x6 -> x4, blocking collectives: 73.5 us -> 52.8 us  [the longest x1 30.6 us: local(): lax.all_gather(jnp.concatenate(mine)[None], ('dp', 'seq'), axis=0)]
    unnamed x126 -> x89, local copies, waits for them, and re-layouts: 17.4 us -> 6.79 us
    reduce_scatter x6 -> x5, waiting for transfers between devices: 122 us -> 113 us  [the longest x4 89.8 us: scatter(): lax.psum_scatter(terms.astype(jnp.bfloat16), 'tensor', scatter_dimension=...]
    dot_general x6, matrix products: 12.8 us -> 5.7 us  [product_cols(): lax.dot_general(left, right, (((1,), (1,)), ((), ())), preferred_element_...]
    convert_element_type x12 -> x18, other arithmetic: 8.56 us -> 14.2 us  [the longest x1 4.69 us: local(): grad_scores = (probs * (grad_probs - inner_sum)).astype(bf16)]
  transfers between devices with their start and end apart: 7 -> 9, of which waited for: 6 -> 9; matrix products, arithmetic and copies ran while one was open for 6% -> 7% of each run, Pallas kernels for 0% -> 0%
where the time goes in v1:
time: 490 us; the launch traced here: 489 us
  waiting for transfers between devices  322 us (66%)
  matrix products  55.6 us (11%)
  blocking collectives  52.8 us (11%)
  other arithmetic  31 us (6%)
  between operations  14.5 us (3%)
  local copies, waits for them, and re-layouts  12.6 us (3%)
    psum x1, waiting for transfers between devices, local(): lax.psum((grad_up.astype(bf16), grad_down.astype(bf16), grad_wout.astype(...  118 us
    reduce_scatter x4, waiting for transfers between devices, scatter(): lax.psum_scatter(terms.astype(jnp.bfloat16), 'tensor', scatter_dimension=...  89.8 us
    all_gather x1, waiting for transfers between devices, local(): lax.all_gather(jnp.concatenate([keys, values], axis=1), 'seq', axis=0, ti...  35.6 us
    psum x1, waiting for transfers between devices, local(): late = lax.psum(grad_qkv, ('dp', 'seq')).astype(f32)  33.4 us
    all_gather x1, blocking collectives, local(): lax.all_gather(jnp.concatenate(mine)[None], ('dp', 'seq'), axis=0)  30.6 us
    reduce_scatter x1, waiting for transfers between devices, local(): lax.psum_scatter(jnp.concatenate([key_terms, value_terms], axis=1).astype...  23.5 us
    all_gather x1, waiting for transfers between devices, local(): lax.all_gather(jnp.concatenate([inputs[0], cotangent[0]], axis=1), 'tenso...  21.3 us
    dot_general x6, matrix products, product(): return jnp.dot(left, right, preferred_element_type=jnp.float32)  12.1 us
  transfers between devices with their start and end apart: 9, of which 9 were waited for; matrix products, arithmetic and copies ran while one was open for 7% of the time, Pallas kernels for 0%

profile of v1, /device:TPU:0, one launch (start us, length us, event | category | flops | bytes accessed | tf_op | source)
XLA Modules:
  0.0 489.1 jit_solution(9461729868237713304)
XLA Ops:
  7.3 1.9 pad_maximum_fusion.1
  9.2 0.7 convert_element_type.185
  9.9 0.7 convert_element_type.181
  10.6 0.7 convert_element_type.182
  11.2 21.3 %all-gather.6.cloned.1.call-done = bf16[512,1536]{1,0:T(8,128)(2,1)} async-done(((bf16[128,1536]{1,0:T(8,128)(2,1)}), bf16[512,1536]{1,0:T(8,128)(2,1)}) %all-gather.6.cloned.1.call-update) | async-done | bytes 1572880 | tf_op jit(solution)/shard_map/all_gather | solution.py:84
  32.6 1.4 convert_reduce_fusion
  34.0 1.9 convert_reduce_fusion.2
  36.3 0.4 convolution_convert_fusion.8
  36.7 0.4 copy-done.12
  37.1 0.4 fusion.25
  37.6 0.8 pad_maximum_fusion.2
  38.4 1.5 fusion.26
  40.0 35.6 %all-gather.8.cloned.1.call-done = bf16[2048,384]{0,1:T(8,128)(2,1)} async-done(((bf16[512,384]{0,1:T(8,128)(2,1)}), bf16[2048,384]{0,1:T(8,128)(2,1)}) %all-gather.8.cloned.1.call-update) | async-done | bytes 1572880 | tf_op jit(solution)/shard_map/all_gather | solution.py:95
  75.6 1.5 fusion.70
  77.1 1.9 multiply_reduce_fusion.1
  79.1 2.5 fusion
  81.6 2.1 copy-done.2
  83.7 3.4 fusion.28
  87.1 0.6 copy-done.23
  87.7 1.3 convolution_convert_fusion.5
  89.3 22.0 %reduce-scatter.6.cloned.1.call-done = bf16[128,768]{1,0:T(8,128)(2,1)} async-done(((bf16[512,768]{1,0:T(8,128)(2,1)}), bf16[128,768]{1,0:T(8,128)(2,1)}) %reduce-scatter.6.cloned.1.call-update) | async-done | bytes 196624 | tf_op jit(solution)/shard_map/reduce_scatter | solution.py:52
  111.3 1.1 fusion.49
  112.4 1.1 multiply_reduce_fusion.2
  113.5 1.1 add_convert_fusion.2
  114.6 8.2 %all_gather.23 = bf16[512,768]{1,0:T(8,128)(2,1)S(1)} all-gather(bf16[128,768]{1,0:T(8,128)(2,1)S(1)} %add_convert_fusion.2), channel_id=1, replica_groups=mesh['dp'=2,'seq'=4,'tensor'=4] {'tensor'}, dimensions={0}, use_global_device_ids=true | all-gather | bytes 983040 | tf_op jit(solution)/shard_map/all_gather | solution.py:115
  122.9 5.2 %multiply_convert_fusion.1 = (bf16[512,768]{1,0:T(8,128)(2,1)}, f32[512,768]{1,0:T(8,128)S(1)}, f32[512,768]{1,0:T(8,128)S(1)}) fusion(f32[768]{0:T(1024)S(1)} %convert_element_type.199, bf16[512,768]{1,0:T(8,128)(2,1)S(1)} %all_gather.23, bf16[768,768]{1,0:T(8,128)(2,1)S(1)} %copy-done), kind=kOutput, calls=%fused_computation.33 | convolution fusion | flops 629932032 | bytes 5901312 | tf_op jit(solution)/shard_map/dot_general | solution.py:16
  128.1 1.2 convert_reduce_fusion.1
  129.3 0.9 copy-done.39
  130.1 1.7 convolution_convert_fusion.3
  131.9 3.2 convolution_convert_fusion.4
  135.5 20.2 %reduce-scatter.10.cloned.1.call-done = bf16[128,768]{1,0:T(8,128)(2,1)} async-done(((bf16[512,768]{1,0:T(8,128)(2,1)}), bf16[128,768]{1,0:T(8,128)(2,1)}) %reduce-scatter.10.cloned.1.call-update) | async-done | bytes 196624 | tf_op jit(solution)/shard_map/reduce_scatter | solution.py:52
  155.7 1.2 fusion.55
  156.9 24.9 %reduce-scatter.8.cloned.1.call-done = bf16[128,768]{1,0:T(8,128)(2,1)} async-done(((bf16[512,768]{1,0:T(8,128)(2,1)}), bf16[128,768]{1,0:T(8,128)(2,1)}) %reduce-scatter.8.cloned.1.call-update) | async-done | bytes 196624 | tf_op jit(solution)/shard_map/reduce_scatter | solution.py:52
  181.9 2.0 fusion.67
  184.0 8.7 %all-gather = bf16[576,768]{1,0:T(8,128)(2,1)S(1)} all-gather(bf16[144,768]{1,0:T(8,128)(2,1)S(1)} %maximum_maximum_fusion), channel_id=2, replica_groups=mesh['dp'=2,'seq'=4,'tensor'=4] {'tensor'}, dimensions={0}, use_global_device_ids=true | all-gather | bytes 1105920 | tf_op jit(solution)/shard_map/all_gather | solution.py:129
  193.2 0.5 copy-done.7
  193.7 7.9 %fusion.8 = bf16[3,64,2048]{2,1,0:T(8,128)(2,1)} fusion(bf16[512,3,64]{0,2,1:T(8,128)(2,1)S(1)} %bitcast.93, f32[3,512,2048]{2,1,0:T(8,128)} %copy-done.2, f32[3,512]{1,0:T(4,128)S(1)} %log_add_fusion), kind=kOutput, calls=%fused_computation.14 | convolution fusion | flops 412483584 | bytes 13572096 | tf_op jit(solution)/shard_map/hqk,qhd->khd/dot_general | solution.py:152
  201.7 6.6 %multiply_reduce_fusion = (f32[3,512]{1,0:T(4,128)S(1)}, f32[3,512,2048]{2,1,0:T(8,128)S(1)}) fusion(f32[3,512,2048]{2,1,0:T(8,128)} %copy-done.2, f32[3,512]{1,0:T(4,128)S(1)} %log_add_fusion, bf16[512,3,64]{0,2,1:T(8,128)(2,1)S(1)} %bitcast.94, bf16[2048,3,64]{0,2,1:T(8,128)(2,1)S(1)} %bitcast.90), kind=kOutput, calls=%fused_computation.1 | convolution fusion | flops 415234560 | bytes 26161152 | tf_op jit(solution)/shard_map/qhd,khd->hqk/dot_general | solution.py:147
  208.3 0.4 slice-done.2
  208.8 4.7 multiply_convert_fusion
  213.4 4.1 fusion.7
  217.5 1.2 pad_maximum_fusion
  218.9 3.3 convolution_convert_fusion.1
  222.1 1.9 convolution_convert_fusion
  224.0 1.0 convolution_convert_fusion.6
  225.2 1.0 copy-done.6
  226.2 4.9 %convert_reduce_fusion.7 = (f32[3,64]{1,0:T(4,128)S(1)}, bf16[3,64,512]{2,1,0:T(8,128)(2,1)S(1)}) fusion(bf16[2048,3,64]{0,2,1:T(8,128)(2,1)S(1)} %bitcast.83, bf16[3,512,2048]{2,1,0:T(8,128)(2,1)} %multiply_convert_fusion), kind=kOutput, calls=%fused_computation.98 | convolution fusion | flops 403046208 | bytes 7275264 | tf_op jit(solution)/shard_map/hqk,khd->qhd/dot_general | solution.py:160
  231.1 23.5 %reduce-scatter.12.cloned.1.call-done = bf16[512,384]{0,1:T(8,128)(2,1)} async-done(((bf16[2048,384]{0,1:T(8,128)(2,1)}), bf16[512,384]{0,1:T(8,128)(2,1)}) %reduce-scatter.12.cloned.1.call-update) | async-done | bytes 393232 | tf_op jit(solution)/shard_map/reduce_scatter | solution.py:154
  254.7 2.8 convolution_convert_fusion.2
  257.5 118.0 %all-reduce.6.cloned.1.call-done = (bf16[768,768]{1,0:T(8,128)(2,1)}, bf16[768,768]{1,0:T(8,128)(2,1)}, bf16[192,768]{1,0:T(8,128)(2,1)}) async-done(((bf16[768,768]{1,0:T(8,128)(2,1)}, bf16[768,768]{1,0:T(8,128)(2,1)}, bf16[192,768]{1,0:T(8,128)(2,1)}), (bf16[768,768]{1,0:T(8,128)(2,1)}, bf16[768,768]{1,0:T(8,128)(2,1)}, bf16[192,768]{1,0:T(8,128)(2,1)})) %all-reduce.6.cloned.1.call-update) | async-done | bytes 2654224 | tf_op jit(solution)/shard_map/psum | solution.py:138
  376.8 1.6 fusion.17
  378.9 0.5 copy-done.29
  379.4 0.9 convert_element_type.233
  380.3 5.2 %all_gather.26 = f32[4,8,192]{2,1,0:T(8,128)S(1)} all-gather(f32[1,8,192]{2,1,0:T(8,128)S(1)} %all_gather_reshape.3), channel_id=1, replica_groups=mesh['dp'=2,'seq'=4,'tensor'=4] {'tensor'}, dimensions={0}, use_global_device_ids=true | all-gather | bytes 30720 | tf_op jit(solution)/shard_map/all_gather | solution.py:178
  385.7 30.6 %all-gather.2 = f32[8,1,2304]{2,1,0:T(1,128)S(1)} all-gather(f32[1,1,2304]{2,1,0:T(1,128)S(1)} %reshape.153), channel_id=3, replica_groups=mesh['dp'=2,'seq'=4,'tensor'=4] {'dp','seq'}, dimensions={0}, use_global_device_ids=true | all-gather | bytes 82944 | tf_op jit(solution)/shard_map/all_gather | solution.py:193
  416.4 0.6 split.43
  417.0 1.6 convert_element_type.234
  418.7 1.6 convert_element_type.235
  420.3 0.7 fusion.72
  420.9 33.4 %all-reduce.4.cloned.1.call-done = bf16[768,576]{0,1:T(8,128)(2,1)} async-done(((bf16[768,576]{0,1:T(8,128)(2,1)}), bf16[768,576]{0,1:T(8,128)(2,1)}) %all-reduce.4.cloned.1.call-update) | async-done | bytes 884752 | tf_op jit(solution)/shard_map/psum | solution.py:172
  454.4 2.5 fusion.71
  456.8 22.7 %reduce-scatter.14.cloned.1.call-done = bf16[128,768]{1,0:T(8,128)(2,1)} async-done(((bf16[512,768]{1,0:T(8,128)(2,1)}), bf16[128,768]{1,0:T(8,128)(2,1)}) %reduce-scatter.14.cloned.1.call-update) | async-done | bytes 196624 | tf_op jit(solution)/shard_map/reduce_scatter | solution.py:52
  479.6 1.1 fusion.56
  480.8 1.8 fusion.58
  (145 shorter events, 4.2 us)
Async XLA Ops:
  7.2 115.7 %copy-start = (bf16[768,768]{1,0:T(8,128)(2,1)S(1)}, bf16[768,768]{1,0:T(8,128)(2,1)}, u32[]{:S(2)}) copy-start(bf16[768,768]{1,0:T(8,128)(2,1)} %param.29) | copy-start | bytes 3538948
  7.2 25.4 %all-gather.6.cloned.1.call-start = ((), (), s32[]{:S(2)}) async-start(), calls=%async_computation.5 | async-start | bytes 1966080 | tf_op jit(solution)/shard_map/all_gather | solution.py:84
  9.2 66.5 %all-gather.8.cloned.1.call-start = ((), (), s32[]{:S(2)}) async-start(), calls=%async_computation.6 | async-start | bytes 1966080 | tf_op jit(solution)/shard_map/all_gather | solution.py:95
  32.6 3.3 copy-start.4
  34.0 2.3 copy-start.18
  35.9 1.3 copy-start.27
  36.3 0.9 copy-start.12
  36.3 2.1 copy-start.38
  36.3 2.1 copy-start.30
  38.4 72.9 %reduce-scatter.6.cloned.1.call-start = ((), (), s32[]{:S(2)}) async-start(), calls=%async_computation.7 | async-start | bytes 983040 | tf_op jit(solution)/shard_map/reduce_scatter | solution.py:52
  40.0 37.1 %copy-start.20 = (bf16[512,192]{0,1:T(8,128)(2,1)}, bf16[512,192]{0,1:T(8,128)(2,1)S(1)}, u32[]{:S(2)}) copy-start(bf16[512,192]{0,1:T(8,128)(2,1)S(1)} %fusion.26) | copy-start | bytes 589828
  77.1 2.0 copy-start.5
  77.1 4.4 copy-start.10
  79.1 4.6 copy-start.2
  83.7 4.1 copy-start.17
  87.0 0.7 copy-start.23
  87.0 2.0 copy-start.32
  87.1 2.0 copy-start.33
  87.1 2.1 copy-start.34
  87.1 2.1 copy-start.35
  87.1 2.1 copy-start.3
  89.0 66.6 %reduce-scatter.10.cloned.1.call-start = ((), (), s32[]{:S(2)}) async-start(), calls=%async_computation.9 | async-start | bytes 983040 | tf_op jit(solution)/shard_map/reduce_scatter | solution.py:52
  122.9 5.2 %copy-start.25 = (bf16[512,768]{1,0:T(8,128)(2,1)}, bf16[512,768]{1,0:T(8,128)(2,1)S(1)}, u32[]{:S(2)}) copy-start(bf16[512,768]{1,0:T(8,128)(2,1)S(1)} %all_gather.23) | copy-start | bytes 2359300
  122.9 5.2 %copy-start.37 = (bf16[768,768]{1,0:T(8,128)(2,1)S(1)}, bf16[768,768]{1,0:T(8,128)(2,1)}, u32[]{:S(2)}) copy-start(bf16[768,768]{1,0:T(8,128)(2,1)} %param.31) | copy-start | bytes 3538948
  129.2 0.9 copy-start.39
  131.8 50.0 %reduce-scatter.8.cloned.1.call-start = ((), (), s32[]{:S(2)}) async-start(), calls=%async_computation.8 | async-start | bytes 983040 | tf_op jit(solution)/shard_map/reduce_scatter | solution.py:52
  131.9 3.5 copy-start.36
  131.9 23.8 %copy-start.9 = (bf16[128,768]{1,0:T(8,128)(2,1)S(1)}, bf16[128,768]{1,0:T(8,128)(2,1)}, u32[]{:S(2)}) copy-start(bf16[128,768]{1,0:T(8,128)(2,1)} %reduce-scatter.6.cloned.1.call-done) | copy-start | bytes 589828
  135.1 46.7 %copy-start.26 = (bf16[1,128,768]{2,1,0:T(8,128)(2,1)S(1)}, bf16[1,128,768]{2,1,0:T(8,128)(2,1)}, u32[]{:S(2)}) copy-start(bf16[1,128,768]{2,1,0:T(8,128)(2,1)} %param.33) | copy-start | bytes 589828
  135.2 119.5 %reduce-scatter.12.cloned.1.call-start = ((), (), s32[]{:S(2)}) async-start(), calls=%async_computation.10 | async-start | bytes 1966080 | tf_op jit(solution)/shard_map/reduce_scatter | solution.py:154
  192.8 1.0 copy-start.7
  193.7 7.9 %copy-start.11 = (bf16[2048,192]{0,1:T(8,128)(2,1)S(1)}, bf16[2048,192]{0,1:T(8,128)(2,1)}, u32[]{:S(2)}) copy-start(bf16[2048,192]{0,1:T(8,128)(2,1)} %copy-done.10) | copy-start | bytes 2359300
  193.7 14.6 %slice-start = ((s8[12582912]{0:T(1024)(128)(4,1)}), s8[4194304]{0:T(1024)(128)(4,1)S(1)}, s32[]{:S(2)}) async-start(s8[12582912]{0:T(1024)(128)(4,1)} %bitcast.79), calls=%async_computation.14 | async-start | bytes 8388608
  201.7 6.6 %slice-start.1 = ((s8[12582912]{0:T(1024)(128)(4,1)}), s8[4194304]{0:T(1024)(128)(4,1)S(1)}, s32[]{:S(2)}) async-start(s8[12582912]{0:T(1024)(128)(4,1)} %bitcast.79), calls=%async_computation.15 | async-start | bytes 8388608
  201.7 7.1 %slice-start.2 = ((s8[12582912]{0:T(1024)(128)(4,1)}), s8[4194304]{0:T(1024)(128)(4,1)S(1)}, s32[]{:S(2)}) async-start(s8[12582912]{0:T(1024)(128)(4,1)} %bitcast.79), calls=%async_computation.16 | async-start | bytes 8388608
  208.8 4.7 copy-start.21
  213.4 4.1 copy-start.13
  218.8 156.7 %all-reduce.6.cloned.1.call-start = ((), (), s32[]{:S(2)}) async-start(), calls=%async_computation.13 | async-start | bytes 5308416 | tf_op jit(solution)/shard_map/psum | solution.py:138
  218.8 3.3 copy-start.40
  222.1 1.9 copy-start.24
  225.1 1.2 copy-start.6
  225.1 229.3 %all-reduce.4.cloned.1.call-start = ((), (), s32[]{:S(2)}) async-start(), calls=%async_computation.12 | async-start | bytes 1769472 | tf_op jit(solution)/shard_map/psum | solution.py:172
  254.7 121.2 %copy-start.31 = (bf16[768,192]{0,1:T(8,128)(2,1)S(1)}, bf16[768,192]{0,1:T(8,128)(2,1)}, u32[]{:S(2)}) copy-start(bf16[768,192]{0,1:T(8,128)(2,1)} %param.20) | copy-start | bytes 884740
  257.5 118.8 %copy-start.19 = (bf16[768,192]{0,1:T(8,128)(2,1)S(1)}, bf16[768,192]{0,1:T(8,128)(2,1)}, u32[]{:S(2)}) copy-start(bf16[768,192]{0,1:T(8,128)(2,1)} %param.22) | copy-start | bytes 884740
  257.5 118.8 %copy-start.22 = (bf16[512,384]{0,1:T(8,128)(2,1)S(1)}, bf16[512,384]{0,1:T(8,128)(2,1)}, u32[]{:S(2)}) copy-start(bf16[512,384]{0,1:T(8,128)(2,1)} %reduce-scatter.12.cloned.1.call-done) | copy-start | bytes 1179652
  375.5 104.0 %reduce-scatter.14.cloned.1.call-start = ((), (), s32[]{:S(2)}) async-start(), calls=%async_computation.11 | async-start | bytes 983040 | tf_op jit(solution)/shard_map/reduce_scatter | solution.py:52
  375.8 1.0 copy-start.28
  376.8 1.7 copy-start.8
  378.4 1.0 copy-start.29
  378.4 38.6 %copy-start.16 = (bf16[768,768]{1,0:T(8,128)(2,1)S(1)}, bf16[768,768]{1,0:T(8,128)(2,1)}, u32[]{:S(2)}) copy-start(bf16[768,768]{1,0:T(8,128)(2,1)} %get-tuple-element.23) | copy-start | bytes 3538948
  417.0 1.7 copy-start.15
  420.9 59.8 %copy-start.14 = (f32[128,768]{1,0:T(8,128)S(1)}, f32[128,768]{1,0:T(8,128)}, u32[]{:S(2)}) copy-start(f32[128,768]{1,0:T(8,128)} %get-tuple-element.41) | copy-start | bytes 1179652
  454.4 28.2 %copy-start.1 = (bf16[768,768]{1,0:T(8,128)(2,1)S(1)}, bf16[768,768]{1,0:T(8,128)(2,1)}, u32[]{:S(2)}) copy-start(bf16[768,768]{1,0:T(8,128)(2,1)} %param.29) | copy-start | bytes 3538948
Sparse Core Ops, SparseCore 0:
  10.2 22.3 all-gather.5
  38.5 37.0 all-gather.7
  89.2 22.0 reduce-scatter.5
  132.0 23.6 reduce-scatter.9
  158.6 23.2 reduce-scatter.7
  218.9 35.6 reduce-scatter.11
  259.6 115.8 all-reduce.5
  379.4 74.9 all-reduce.3
  457.1 22.4 reduce-scatter.13

commit v2 on v1

--- a/solution.py
+++ b/solution.py
@@ -4,6 +4,8 @@
 import jax.numpy as jnp
 import numpy as np
 from jax import lax
+from jax.experimental import pallas as pl
+from jax.experimental.pallas import tpu as pltpu
 from jax.sharding import PartitionSpec as P
 
 HEAD_DIM = 64
@@ -48,9 +50,348 @@
     return lax.dynamic_slice_in_dim(vector, rank * share, share, 0)
 
 
-def scatter(terms):
-    return lax.psum_scatter(
-        terms.astype(jnp.bfloat16), "tensor", scatter_dimension=0, tiled=True
+def as_rows(values, multiple):
+    pad = -values.shape[-1] % (128 * multiple)
+    values = jnp.pad(values, [(0, 0)] * (values.ndim - 1) + [(0, pad)])
+    return values.reshape(*values.shape[:-1], -1, 128)
+
+
+def call(kernel, number, out_shape, scratch, bytes_moved, *operands):
+    vmem = pl.BlockSpec(memory_space=pltpu.VMEM)
+    return pl.pallas_call(
+        kernel,
+        out_shape=out_shape,
+        in_specs=[vmem] * len(operands),
+        out_specs=jax.tree.map(lambda _: vmem, out_shape),
+        scratch_shapes=scratch,
+        compiler_params=pltpu.CompilerParams(
+            collective_id=number, has_side_effects=True, vmem_limit_bytes=40 * 2**20
+        ),
+        cost_estimate=pl.CostEstimate(flops=0, bytes_accessed=bytes_moved, transcendentals=0),
+    )(*operands)
+
+
+def greet(peers):
+    barrier = pltpu.get_barrier_semaphore()
+    for peer in peers:
+        pl.semaphore_signal(barrier, inc=1, device_id=peer, device_id_type=pl.DeviceIdType.MESH)
+    pl.semaphore_wait(barrier, len(peers))
+
+
+def send(source, target, sems, slot, peer):
+    return pltpu.make_async_remote_copy(
+        src_ref=source,
+        dst_ref=target,
+        send_sem=sems[0].at[slot],
+        recv_sem=sems[1].at[slot],
+        device_id=peer,
+        device_id_type=pl.DeviceIdType.MESH,
+    )
+
+
+def peers_along(axis, n):
+    me = lax.axis_index(axis)
+    return [{axis: lax.rem(me + step, n)} for step in range(1, n)]
+
+
+def block(ref, index, rows):
+    return ref.at[pl.ds(pl.multiple_of(index * rows, 16), rows)]
+
+
+def gather_kernel(n, x, out, *sems):
+    rows = x.shape[0]
+    me = lax.axis_index("tensor")
+    peers = peers_along("tensor", n)
+    greet(peers)
+    copies = [
+        send(x, block(out, me, rows), sems, step, peer) for step, peer in enumerate(peers)
+    ]
+    for copy in copies:
+        copy.start()
+    block(out, me, rows)[...] = x[...]
+    for copy in copies:
+        copy.wait()
+
+
+def gather(x, number):
+    n = lax.axis_size("tensor")
+    shape = jax.ShapeDtypeStruct((n * x.shape[0], x.shape[1]), x.dtype)
+    sems = [pltpu.SemaphoreType.DMA((n - 1,))] * 2
+    return call(partial(gather_kernel, n), number, shape, sems, 2**24, x)
+
+
+def scatter_start(n, x, held, sems, peers):
+    rows = x.shape[0] // n
+    me = lax.axis_index("tensor")
+    copies = [
+        send(block(x, lax.rem(me + step + 1, n), rows), held.at[step], sems, step, peer)
+        for step, peer in enumerate(peers)
+    ]
+    for copy in copies:
+        copy.start()
+    return copies
+
+
+def scatter_end(n, x, out, held, copies):
+    rows = x.shape[0] // n
+    total = block(x, lax.axis_index("tensor"), rows)[...].astype(jnp.float32)
+    for step, copy in enumerate(copies):
+        copy.wait_recv()
+        total += held[step].astype(jnp.float32)
+    out[...] = total
+    for copy in copies:
+        copy.wait_send()
+
+
+def scatter_kernel(n, x, out, held, *sems):
+    peers = peers_along("tensor", n)
+    greet(peers)
+    scatter_end(n, x, out, held, scatter_start(n, x, held, sems, peers))
+
+
+def scatter(terms, number):
+    n = lax.axis_size("tensor")
+    rows, width = terms.shape[0] // n, terms.shape[1]
+    return call(
+        partial(scatter_kernel, n),
+        number,
+        jax.ShapeDtypeStruct((rows, width), jnp.float32),
+        [pltpu.VMEM((n - 1, rows, width), jnp.bfloat16)] + [pltpu.SemaphoreType.DMA((n - 1,))] * 2,
+        2**24,
+        terms.astype(jnp.bfloat16),
+    )
+
+
+def line_gather_kernel(n, x, out, *sems):
+    rows = x.shape[0]
+    me = lax.axis_index("seq")
+    greet(peers_along("seq", n))
+    right, left = {"seq": lax.rem(me + 1, n)}, {"seq": lax.rem(me + n - 1, n)}
+    block(out, me, rows)[...] = x[...]
+
+    def hop(step, side):
+        owner = lax.rem(me + (n - step if side == 0 else step), n)
+        here = block(out, owner, rows)
+        return send(here, here, sems[2 * side : 2 * side + 2], step, (right, left)[side])
+
+    for step in range(n - 1):
+        pl.when((me >= step) & (me < n - 1))(lambda: hop(step, 0).start())
+        pl.when((me + step < n) & (me > 0))(lambda: hop(step, 1).start())
+        pl.when(me > step)(lambda: hop(step, 0).wait_recv())
+        pl.when(me + step + 1 < n)(lambda: hop(step, 1).wait_recv())
+    for step in range(n - 1):
+        pl.when((me >= step) & (me < n - 1))(lambda: hop(step, 0).wait_send())
+        pl.when((me + step < n) & (me > 0))(lambda: hop(step, 1).wait_send())
+
+
+def line_gather(x, number):
+    n = lax.axis_size("seq")
+    shape = jax.ShapeDtypeStruct((n * x.shape[0], x.shape[1]), x.dtype)
+    sems = [pltpu.SemaphoreType.DMA((n - 1,))] * 4
+    return call(partial(line_gather_kernel, n), number, shape, sems, 2**25, x)
+
+
+def line_scatter_kernel(n, x, out, held, staged, *sems):
+    rows = x.shape[0] // n
+    me = lax.axis_index("seq")
+    greet(peers_along("seq", n))
+    neighbours = {"seq": lax.rem(me + 1, n)}, {"seq": lax.rem(me + n - 1, n)}
+
+    def hop(step, side):
+        return send(
+            staged.at[side, step],
+            held.at[side, step],
+            sems[2 * side : 2 * side + 2],
+            step,
+            neighbours[side],
+        )
+
+    def advance(step, side):
+        place = me if side == 0 else n - 1 - me
+        mine = x[pl.ds((n - 1 - step if side == 0 else step) * rows, rows), :]
+
+        def first():
+            staged[side, step] = mine
+            hop(step, side).start()
+
+        def later():
+            passing = held[side, step].astype(jnp.float32)
+            staged[side, step] = (mine.astype(jnp.float32) + passing).astype(mine.dtype)
+            hop(step, side).start()
+
+        pl.when((place > 0) & (place <= n - 1 - step))(lambda: hop(step, side).wait_recv())
+        pl.when(place == 0)(first)
+        pl.when((place > 0) & (place < n - 1 - step))(later)
+
+    for step in range(n - 1):
+        advance(step, 0)
+        advance(step, 1)
+    out[...] = block(x, me, rows)[...].astype(jnp.float32)
+
+    def add(side, step):
+        out[...] += held[side, step].astype(jnp.float32)
+
+    for step in range(n - 1):
+        pl.when(me == n - 1 - step)(lambda: add(0, step))
+        pl.when(me == step)(lambda: add(1, step))
+    for step in range(n - 1):
+        pl.when(me < n - 1 - step)(lambda: hop(step, 0).wait_send())
+        pl.when(n - 1 - me < n - 1 - step)(lambda: hop(step, 1).wait_send())
+
+
+def line_scatter(x, number):
+    n = lax.axis_size("seq")
+    rows, width = x.shape[0] // n, x.shape[1]
+    return call(
+        partial(line_scatter_kernel, n),
+        number,
+        jax.ShapeDtypeStruct((rows, width), jnp.float32),
+        [pltpu.VMEM((2, n - 1, rows, width), x.dtype)] * 2
+        + [pltpu.SemaphoreType.DMA((n - 1,))] * 4,
+        2**25,
+        x,
+    )
+
+
+def final_kernel(
+    n,
+    dp,
+    seq,
+    term,
+    mlp,
+    w,
+    v_one,
+    v_two,
+    term_out,
+    mlp_out,
+    w_out,
+    v_out,
+    term_held,
+    mlp_held,
+    w_held,
+    w_total,
+    v_one_held,
+    v_mine,
+    v_held,
+    *sems,
+):
+    f32 = jnp.float32
+    count = dp * seq
+    rows = w.shape[0] // count
+    lane = lax.axis_index("tensor")
+    me = lax.axis_index("dp") * seq + lax.axis_index("seq")
+    near = peers_along("tensor", n)
+
+    def far(step):
+        index = lax.rem(me + step, count)
+        return index, {"dp": index // seq, "seq": lax.rem(index, seq)}
+
+    barrier = pltpu.get_barrier_semaphore()
+
+    def signal(peer):
+        pl.semaphore_signal(barrier, inc=1, device_id=peer, device_id_type=pl.DeviceIdType.MESH)
+
+    for peer in near:
+        signal(peer)
+    pl.loop(1, count)(lambda step: signal(far(step)[1]))
+    pl.semaphore_wait(barrier, n - 1 + count - 1)
+
+    pairs = [sems[i : i + 2] for i in range(0, len(sems), 2)]
+    ones = [
+        send(v_one.at[lax.rem(lane + step + 1, n)], v_one_held.at[step], pairs[0], step, peer)
+        for step, peer in enumerate(near)
+    ]
+    for copy in ones:
+        copy.start()
+
+    def first(step):
+        index, peer = far(step)
+        return send(block(w, index, rows), w_held.at[step - 1], pairs[1], step - 1, peer)
+
+    def second(step):
+        here = block(w_out, me, rows)
+        return send(here, here, pairs[2], step - 1, far(step)[1])
+
+    def vector(step):
+        return send(v_mine, v_held.at[step - 1], pairs[3], step - 1, far(step)[1])
+
+    pl.loop(1, count)(lambda step: first(step).start())
+    terms = scatter_start(n, term, term_held, pairs[4], near)
+    mlps = scatter_start(n, mlp, mlp_held, pairs[5], near)
+    total = v_one[lane]
+    for step, copy in enumerate(ones):
+        copy.wait_recv()
+        total += v_one_held[step]
+    v_mine[0:8, :] = total
+    v_mine[8:, :] = v_two[...]
+    pl.loop(1, count)(lambda step: vector(step).start())
+    w_total[...] = block(w, me, rows)[...].astype(f32)
+
+    @pl.loop(1, count)
+    def _(step):
+        first(step).wait_recv()
+        w_total[...] += w_held[step - 1].astype(f32)
+
+    block(w_out, me, rows)[...] = w_total[...].astype(w_out.dtype)
+    pl.loop(1, count)(lambda step: second(step).start())
+    scatter_end(n, term, term_out, term_held, terms)
+    scatter_end(n, mlp, mlp_out, mlp_held, mlps)
+    v_out[...] = v_mine[...]
+
+    @pl.loop(1, count)
+    def _(step):
+        vector(step).wait_recv()
+        v_out[...] += v_held[step - 1]
+
+    for copy in ones:
+        copy.wait_send()
+
+    @pl.loop(1, count)
+    def _(step):
+        second(step).wait_recv()
+        first(step).wait_send()
+        second(step).wait_send()
+        vector(step).wait_send()
+
+
+def final(term, mlp, w, v_one, v_two, number):
+    n, dp, seq = lax.axis_size("tensor"), lax.axis_size("dp"), lax.axis_size("seq")
+    f32, bf16 = jnp.float32, jnp.bfloat16
+    count = dp * seq
+    pad = -w.shape[0] % (16 * count)
+    w = jnp.pad(w, ((0, pad), (0, 0))) if pad else w
+    rows = term.shape[0] // n
+    vectors = (8 + v_two.shape[0], 128)
+    part = w.shape[0] // count
+    held = pltpu.VMEM((n - 1, rows, term.shape[1]), bf16)
+    near, far = [pltpu.SemaphoreType.DMA((n - 1,))] * 2, [pltpu.SemaphoreType.DMA((count - 1,))] * 2
+    return call(
+        partial(final_kernel, n, dp, seq),
+        number,
+        (
+            jax.ShapeDtypeStruct((rows, term.shape[1]), f32),
+            jax.ShapeDtypeStruct((rows, term.shape[1]), f32),
+            jax.ShapeDtypeStruct(w.shape, bf16),
+            jax.ShapeDtypeStruct(vectors, f32),
+        ),
+        [
+            held,
+            held,
+            pltpu.VMEM((count - 1, part, w.shape[1]), bf16),
+            pltpu.VMEM((part, w.shape[1]), f32),
+            pltpu.VMEM((n - 1, 8, 128), f32),
+            pltpu.VMEM(vectors, f32),
+            pltpu.VMEM((count - 1, *vectors), f32),
+        ]
+        + near
+        + far * 3
+        + near * 2,
+        2**26,
+        term,
+        mlp,
+        w,
+        v_one,
+        v_two,
     )
 
 
@@ -81,9 +422,7 @@
     gain_one = ln1_gain.astype(f32)
     gain_two = ln2_gain.astype(f32)
     frames_in = inputs[0].astype(f32)
-    both = lax.all_gather(
-        jnp.concatenate([inputs[0], cotangent[0]], axis=1), "tensor", axis=0, tiled=True
-    )
+    both = gather(jnp.concatenate([inputs[0], cotangent[0]], axis=1), 1)
     grad_z_all = both[:, width:]
     normed_one, scaled_all, _ = normalize(
         both[:, :width].astype(f32), gain_one, ln1_bias.astype(f32)
@@ -92,7 +431,7 @@
     heads_width = w_query.shape[1]
     keys = product(attn_input, w_key).astype(bf16)
     values = (product(attn_input, w_value) + b_value.astype(f32)).astype(bf16)
-    kv_all = lax.all_gather(jnp.concatenate([keys, values], axis=1), "seq", axis=0, tiled=True)
+    kv_all = line_gather(jnp.concatenate([keys, values], axis=1), 2)
     query = (product(attn_input, w_query) + b_query.astype(f32)).astype(bf16)
     grad_hidden = product_cols(grad_z_all, w_down)
     frames = query.shape[0]
@@ -109,16 +448,16 @@
     weights_low = (expo / total).astype(bf16)
     context = jnp.einsum("hqk,khd->qhd", weights_low, value3, preferred_element_type=f32)
     context = context.reshape(frames, heads_width).astype(bf16)
-    attn_rows = scatter(product(context, w_out)).astype(f32)
+    attn_rows = scatter(product(context, w_out), 3)
     middle = frames_in + attn_rows + b_out.astype(f32)
     normed_two, scaled_two, spread_two = normalize(middle, gain_two, ln2_bias.astype(f32))
-    mlp_input = lax.all_gather(normed_two.astype(bf16), "tensor", axis=0, tiled=True)
+    mlp_input = gather(normed_two.astype(bf16), 4)
     before = product(mlp_input, w_up) + b_up.astype(f32)
     activated, gelu_back = jax.vjp(partial(jax.nn.gelu, approximate=False), before)
     hidden = activated.astype(bf16)
     (grad_before,) = gelu_back(grad_hidden)
     grad_before = grad_before.astype(bf16)
-    grad_two = scatter(product_cols(grad_before, w_up)).astype(f32)
+    grad_two = scatter(product_cols(grad_before, w_up), 5)
     upstream = cotangent[0].astype(f32)
     grad_middle = upstream + normalize_back(grad_two, scaled_two, spread_two, gain_two)
     grad_attn_rows = grad_middle.astype(bf16)
@@ -126,18 +465,17 @@
     high = sums_two.astype(bf16)
     low = (sums_two - high.astype(f32)).astype(bf16)
     extra = jnp.concatenate([high, low, jnp.zeros((12, width), bf16)])
-    packed = lax.all_gather(jnp.concatenate([grad_attn_rows, extra]), "tensor", axis=0)
+    packed = gather(jnp.concatenate([grad_attn_rows, extra]), 6).reshape(lanes, -1, width)
     grad_attn_all = packed[:, :own_rows].reshape(frames, width)
     pair = packed[:, own_rows : own_rows + 4].astype(f32).sum(axis=0)
     pair = lax.dynamic_slice_in_dim(pair[:2] + pair[2:], rank * share, share, 1)
-    mlp_rows = scatter(product(hidden, w_down)).astype(f32)
-    result = (middle + mlp_rows + b_down.astype(f32)).astype(bf16)
+    mlp_terms = product(hidden, w_down).astype(bf16)
     grad_down = product_rows(hidden, grad_z_all)
     grad_up = product_rows(mlp_input, grad_before)
     grad_wout = product_rows(context, grad_attn_all)
-    early = lax.psum(
-        (grad_up.astype(bf16), grad_down.astype(bf16), grad_wout.astype(bf16)), ("dp", "seq")
-    )
+    early = lax.psum((grad_up.astype(bf16), grad_down.astype(bf16)), ("dp", "seq"))
+    grad_wout, early = lax.optimization_barrier((grad_wout.astype(bf16), early))
+    sum_wout = lax.psum(grad_wout, ("dp", "seq"))
     grad_context = (
         product_cols(grad_attn_all, w_out).astype(bf16).reshape(frames, heads, HEAD_DIM)
     )
@@ -151,12 +489,9 @@
     key_terms = key_terms.reshape(kv_all.shape[0], heads_width)
     value_terms = jnp.einsum("hqk,qhd->khd", probs_low, grad_context, preferred_element_type=f32)
     value_terms = value_terms.reshape(kv_all.shape[0], heads_width)
-    grad_kv = lax.psum_scatter(
-        jnp.concatenate([key_terms, value_terms], axis=1).astype(bf16),
-        "seq",
-        scatter_dimension=0,
-        tiled=True,
-    )
+    grad_kv = line_scatter(
+        jnp.concatenate([key_terms, value_terms], axis=1).astype(bf16), 7
+    ).astype(bf16)
     grad_query = jnp.einsum("hqk,khd->qhd", grad_scores, key3, preferred_element_type=f32) * scale
     grad_query = grad_query.reshape(frames, heads_width).astype(bf16)
     grad_keys = grad_kv[:, :heads_width]
@@ -166,21 +501,11 @@
         + product_cols(grad_keys, w_key)
         + product_cols(grad_values, w_value)
     )
-    grad_one = scatter(term).astype(f32)
     grad_qkv = product_rows(attn_input, jnp.concatenate([grad_query, grad_kv], axis=1))
-    grad_qkv, early = lax.optimization_barrier((grad_qkv.astype(bf16), early))
-    late = lax.psum(grad_qkv, ("dp", "seq")).astype(f32)
-    scaled_one, spread_one = normalize(frames_in, gain_one, ln1_bias.astype(f32))[1:]
-    grad_input = (grad_middle + normalize_back(grad_one, scaled_one, spread_one, gain_one)).astype(
-        bf16
-    )
-    sums_one = jnp.concatenate([jnp.sum(term * scaled_all, axis=0), jnp.sum(term, axis=0)])
-    sums_one = lax.all_gather(sums_one.reshape(-1, share), "tensor", axis=0)
-    sums_one = sums_one.sum(axis=0).reshape(2, lanes, share)
-    sums_one = lax.dynamic_index_in_dim(sums_one, rank, 1, keepdims=False)
+    sums_one = jnp.stack([jnp.sum(term * scaled_all, axis=0), jnp.sum(term, axis=0)])
+    v_one = sums_one.reshape(2, lanes, share).swapaxes(0, 1).reshape(lanes, -1)
+    v_one = as_rows(v_one, 8)
     mine = [
-        sums_one[0],
-        sums_one[1],
         jnp.sum(grad_query.astype(f32), axis=0),
         jnp.sum(grad_values.astype(f32), axis=0),
         own_columns(jnp.sum(grad_attn_all.astype(f32), axis=0), rank, share),
@@ -189,9 +514,23 @@
         own_columns(jnp.sum(grad_z_all.astype(f32), axis=0), rank, share),
         jnp.sum(grad_before.astype(f32), axis=0),
     ]
-    ends = np.cumsum([part.shape[0] for part in mine])[:-1]
-    totals = lax.all_gather(jnp.concatenate(mine)[None], ("dp", "seq"), axis=0).sum(axis=(0, 1))
-    gain1, bias1, bq, bv, bo, gain2, bias2, bd, bu = jnp.split(totals, ends)
+    ends = np.cumsum([part.shape[0] for part in mine])
+    grad_one, mlp_rows, late, totals = final(
+        term.astype(bf16),
+        mlp_terms,
+        grad_qkv.astype(bf16),
+        v_one,
+        as_rows(jnp.concatenate(mine), 16),
+        8,
+    )
+    result = (middle + mlp_rows + b_down.astype(f32)).astype(bf16)
+    late = late[:width].astype(f32)
+    gain1, bias1 = totals[:8].reshape(-1)[: 2 * share].reshape(2, share)
+    bq, bv, bo, gain2, bias2, bd, bu = jnp.split(totals[8:].reshape(-1)[: ends[-1]], ends[:-1])
+    scaled_one, spread_one = normalize(frames_in, gain_one, ln1_bias.astype(f32))[1:]
+    grad_input = (grad_middle + normalize_back(grad_one, scaled_one, spread_one, gain_one)).astype(
+        bf16
+    )
     return (
         result[None],
         grad_input[None],
@@ -202,7 +541,7 @@
         late[:, heads_width : 2 * heads_width],
         late[:, 2 * heads_width :],
         bv,
-        early[2].astype(f32),
+        sum_wout.astype(f32),
         bo,
         gain2,
         bias2,

time: 490 us -> 456 us (0.931)
  waiting for transfers between devices: 322 us -> 64.9 us
  Pallas kernels: 0 us -> 254 us
  blocking collectives: 52.8 us -> 0 us
  local copies, waits for them, and re-layouts: 12.6 us -> 33 us
    pallas_call x0 -> x8, Pallas kernels: none -> 254 us  [call(): pl.pallas_call(kernel, out_shape=out_shape, in_specs=[vmem] * len(operand...]
    reduce_scatter x5 -> x0, waiting for transfers between devices: 113 us -> none  [the longest x4 89.8 us: scatter(): lax.psum_scatter(terms.astype(jnp.bfloat16), 'tensor', scatter_dimension=...]
    psum x2, waiting for transfers between devices: 151 us -> 64.9 us  [the longest x1 64.9 us: local(): sum_wout = lax.psum(grad_wout, ('dp', 'seq'))]
    all_gather x2 -> x0, waiting for transfers between devices: 56.9 us -> none  [the longest x1 35.6 us: local(): lax.all_gather(jnp.concatenate([keys, values], axis=1), 'seq', axis=0, ti...]
    all_gather x4 -> x0, blocking collectives: 52.8 us -> none  [the longest x1 30.6 us: local(): lax.all_gather(jnp.concatenate(mine)[None], ('dp', 'seq'), axis=0)]
    unnamed x89 -> x119, local copies, waits for them, and re-layouts: 6.79 us -> 10.1 us
  transfers between devices with their start and end apart: 9 -> 2, of which waited for: 9 -> 1; matrix products, arithmetic and copies ran while one was open for 7% -> 15% of each run, Pallas kernels for 0% -> 39%
where the time goes in v2:
time: 456 us; the launch traced here: 455 us
  Pallas kernels  254 us (56%)
  waiting for transfers between devices  64.9 us (14%)
  matrix products  59.6 us (13%)
  local copies, waits for them, and re-layouts  33 us (7%)
  other arithmetic  28.5 us (6%)
  between operations  14.9 us (3%)
    pallas_call x8, Pallas kernels, call(): pl.pallas_call(kernel, out_shape=out_shape, in_specs=[vmem] * len(operand...  254 us
    psum x1, waiting for transfers between devices, local(): sum_wout = lax.psum(grad_wout, ('dp', 'seq'))  64.9 us
    dot_general x6, matrix products, product(): return jnp.dot(left, right, preferred_element_type=jnp.float32)  16.7 us
    dot_general x6, matrix products, product_cols(): lax.dot_general(left, right, (((1,), (1,)), ((), ())), preferred_element_...  10.5 us
    unnamed x119, local copies, waits for them, and re-layouts  10.1 us
  transfers between devices with their start and end apart: 2, of which 1 were waited for; matrix products, arithmetic and copies ran while one was open for 15% of the time, Pallas kernels for 39%

profile of v2, /device:TPU:0, one launch (start us, length us, event | category | flops | bytes accessed | tf_op | source)
XLA Modules:
  0.0 455.5 jit_solution(8304670381648257959)
XLA Ops:
  7.3 1.4 convert_element_type.189
  10.0 1.0 convert_reduce_fusion.4
  11.0 1.1 pad_maximum_fusion.1.x
  12.1 20.5 %shard_map.296 = bf16[512,1536]{1,0:T(8,128)(2,1)S(1)} custom-call(bf16[128,1536]{1,0:T(8,128)(2,1)S(1)} %pad_maximum_fusion.1.x), custom_call_target="tpu_custom_call" | custom-call | bytes 16777216 | tf_op jit(solution)/shard_map/pallas_call | solution.py:61
  32.8 1.0 convert_reduce_fusion.2
  34.8 1.1 convolution_convert_fusion.8
  35.9 1.8 copy.60
  37.6 1.4 fusion.25
  39.2 34.0 %shard_map.297 = bf16[2048,384]{1,0:T(8,128)(2,1)S(1)} custom-call(bf16[512,384]{1,0:T(8,128)(2,1)S(1)} %pad_maximum_fusion.2.x), custom_call_target="tpu_custom_call" | custom-call | bytes 33554432 | tf_op jit(solution)/shard_map/pallas_call | solution.py:61
  73.2 1.8 fusion.61
  75.0 2.2 copy.61
  77.2 1.4 copy.62
  78.7 1.9 fusion.26
  80.6 1.9 multiply_reduce_fusion.1
  82.5 2.5 fusion
  85.0 2.0 copy-done.4
  87.1 3.4 fusion.28
  90.9 10.3 %shard_map.298 = f32[128,768]{1,0:T(8,128)S(1)} custom-call(bf16[512,768]{1,0:T(8,128)(2,1)S(1)} %convolution_convert_fusion.5.x), custom_call_target="tpu_custom_call" | custom-call | bytes 16777216 | tf_op jit(solution)/shard_map/pallas_call | solution.py:61
  102.4 11.0 %shard_map.299 = bf16[512,768]{1,0:T(8,128)(2,1)S(1)} custom-call(bf16[128,768]{1,0:T(8,128)(2,1)S(1)} %add_convert_fusion.2.x), custom_call_target="tpu_custom_call" | custom-call | bytes 16777216 | tf_op jit(solution)/shard_map/pallas_call | solution.py:61
  113.5 10.2 %multiply_convert_fusion.1 = (bf16[512,768]{1,0:T(8,128)(2,1)S(1)}, f32[512,768]{1,0:T(8,128)S(1)}, f32[512,768]{1,0:T(8,128)S(1)}) fusion(f32[768]{0:T(1024)S(1)} %convert_element_type.194, bf16[512,768]{1,0:T(8,128)(2,1)S(1)} %shard_map.299, bf16[768,768]{1,0:T(8,128)(2,1)S(1)} %copy-done), kind=kOutput, calls=%fused_computation.31 | convolution fusion | flops 629932032 | bytes 5901312 | tf_op jit(solution)/shard_map/dot_general | solution.py:18
  123.7 1.7 convert_reduce_fusion.1
  125.5 1.9 convolution_convert_fusion.1
  127.4 1.8 convolution_convert_fusion
  129.5 2.1 convolution_convert_fusion.4.x
  131.6 11.0 %shard_map.300 = f32[128,768]{1,0:T(8,128)S(1)} custom-call(bf16[512,768]{1,0:T(8,128)(2,1)S(1)} %convolution_convert_fusion.4.x), custom_call_target="tpu_custom_call" | custom-call | bytes 16777216 | tf_op jit(solution)/shard_map/pallas_call | solution.py:61
  143.0 0.9 fusion.58
  144.1 12.5 %shard_map.301 = bf16[576,768]{1,0:T(8,128)(2,1)S(1)} custom-call(bf16[144,768]{1,0:T(8,128)(2,1)S(1)} %maximum_maximum_fusion.x), custom_call_target="tpu_custom_call" | custom-call | bytes 16777216 | tf_op jit(solution)/shard_map/pallas_call | solution.py:61
  157.5 8.0 %fusion.8 = bf16[3,64,2048]{2,1,0:T(8,128)(2,1)} fusion(bf16[512,3,64]{0,2,1:T(8,128)(2,1)S(1)} %bitcast.101, f32[3,512,2048]{2,1,0:T(8,128)} %copy-done.4, f32[3,512]{1,0:T(4,128)S(1)} %log_add_fusion), kind=kOutput, calls=%fused_computation.14 | convolution fusion | flops 412483584 | bytes 13572096 | tf_op jit(solution)/shard_map/hqk,qhd->khd/dot_general | solution.py:490
  165.6 4.6 %multiply_reduce_fusion = (f32[3,512]{1,0:T(4,128)S(1)}, f32[3,512,2048]{2,1,0:T(8,128)S(1)}) fusion(f32[3,512,2048]{2,1,0:T(8,128)S(1)} %bitcast.91, f32[3,512]{1,0:T(4,128)S(1)} %log_add_fusion, bf16[512,3,64]{0,2,1:T(8,128)(2,1)S(1)} %bitcast.102, bf16[2048,3,64]{0,2,1:T(8,128)(2,1)} %bitcast.97), kind=kOutput, calls=%fused_computation.1 | convolution fusion | flops 415234560 | bytes 26161152 | tf_op jit(solution)/shard_map/qhd,khd->hqk/dot_general | solution.py:485
  170.2 4.7 %multiply_convert_fusion = bf16[3,512,2048]{2,1,0:T(8,128)(2,1)} fusion(f32[3,512,2048]{2,1,0:T(8,128)S(1)} %get-tuple-element.123, f32[3,512,2048]{2,1,0:T(8,128)S(1)} %bitcast.91, f32[3,512]{1,0:T(4,128)S(1)} %get-tuple-element.122, f32[3,512]{1,0:T(4,128)S(1)} %log_add_fusion), kind=kLoop, calls=%fused_computation | loop fusion | flops 15728640 | bytes 31469568 | tf_op jit(solution)/shard_map/convert_element_type | solution.py:487
  174.9 5.1 %fusion.7 = bf16[3,64,2048]{2,1,0:T(8,128)(2,1)} fusion(bf16[512,3,64]{0,2,1:T(8,128)(2,1)S(1)} %bitcast.106, bf16[3,512,2048]{2,1,0:T(8,128)(2,1)} %multiply_convert_fusion), kind=kOutput, calls=%fused_computation.13 | convolution fusion | flops 403439616 | bytes 7274496 | tf_op jit(solution)/shard_map/hqk,qhd->khd/dot_general | solution.py:488
  180.0 2.7 convert_reduce_fusion.6
  182.7 1.7 convolution_convert_fusion.3.mlp
  184.4 1.6 fusion.67
  186.0 0.8 copy.65
  186.8 2.2 copy.64
  189.0 2.2 copy.63
  191.2 2.2 pad_maximum_fusion.x
  193.4 104.3 %shard_map.302 = f32[512,384]{1,0:T(8,128)S(1)} custom-call(bf16[2048,384]{1,0:T(8,128)(2,1)S(1)} %pad_maximum_fusion.x), custom_call_target="tpu_custom_call" | custom-call | bytes 33554432 | tf_op jit(solution)/shard_map/pallas_call | solution.py:61
  297.8 1.5 fusion.48
  299.3 0.7 convert_reduce_fusion.5
  300.1 0.7 convert_reduce_fusion.3
  301.4 1.9 convolution_convert_fusion.2
  303.3 2.3 copy.66.w
  305.6 3.2 fusion.17
  308.8 0.8 stack.22
  309.8 0.7 reduce_sum.213
  310.6 0.8 fusion.63
  311.4 0.8 dynamic_slice.9
  312.2 0.8 dynamic_slice.11
  313.6 0.8 concatenate.25
  314.4 1.2 copy-done.2
  315.6 1.1 copy-done.3
  316.8 50.8 %shard_map.303 = (f32[128,768]{1,0:T(8,128)S(1)}, f32[128,768]{1,0:T(8,128)S(1)}, bf16[768,576]{1,0:T(8,128)(2,1)S(1)}, f32[24,128]{1,0:T(8,128)S(1)}) custom-call(bf16[512,768]{1,0:T(8,128)(2,1)S(1)} %get-tuple-element.100.term, bf16[512,768]{1,0:T(8,128)(2,1)S(1)} %copy-done.3, bf16[768,576]{1,0:T(8,128)(2,1)S(1)} %copy-done.2, f32[4,8,128]{2,1,0:T(8,128)S(1)} %bitcast.89, ...), custom_call_target="tpu_custom_call" | custom-call | bytes 67108864 | tf_op jit(solution)/shard_map/pallas_call | solution.py:61
  370.5 1.1 convolution_convert_fusion.6
  371.5 1.4 fusion.62
  373.0 2.3 copy.67
  375.2 1.1 copy.68
  376.3 1.1 copy.69
  377.4 0.9 fusion.52
  378.7 1.6 convert_element_type.226
  380.4 1.6 convert_element_type.227
  382.0 64.9 %all-reduce.6.cloned.1.call-done = bf16[192,768]{1,0:T(8,128)(2,1)} async-done(((bf16[192,768]{1,0:T(8,128)(2,1)}), bf16[192,768]{1,0:T(8,128)(2,1)}) %all-reduce.6.cloned.1.call-update) | async-done | bytes 294928 | tf_op jit(solution)/shard_map/psum | solution.py:478
  446.8 1.8 convert_element_type.225
  (170 shorter events, 11.1 us)
Async XLA Ops:
  7.2 106.3 %copy-start = (bf16[768,768]{1,0:T(8,128)(2,1)S(1)}, bf16[768,768]{1,0:T(8,128)(2,1)}, u32[]{:S(2)}) copy-start(bf16[768,768]{1,0:T(8,128)(2,1)} %param.29) | copy-start | bytes 3538948
  7.2 365.7 %all-reduce.8.cloned.1.call-start = ((), (), s32[]{:S(2)}) async-start(), calls=%async_computation.1 | async-start | bytes 4718592 | tf_op jit(solution)/shard_map/psum | solution.py:476
  32.6 1.3 copy-start.49
  32.8 2.0 copy-start.30
  32.8 2.0 copy-start.22
  33.8 3.8 copy-start.34
  34.8 4.3 copy-start.14
  37.6 1.4 copy-start.26
  75.0 2.2 copy-start.50
  78.7 3.8 copy-start.6
  80.6 1.9 copy-start.24
  82.5 4.5 copy-start.4
  82.5 4.5 copy-start.11
  85.0 5.4 %copy-start.32 = (f32[3,512]{1,0:T(4,128)}, f32[3,512]{1,0:T(4,128)S(1)}, u32[]{:S(2)}) copy-start(f32[3,512]{1,0:T(4,128)S(1)} %fusion) | copy-start | bytes 18436
  87.1 3.5 copy-start.20
  90.4 10.8 %copy-start.43 = (bf16[768]{0:T(1024)(128)(2,1)S(1)}, bf16[768]{0:T(1024)(128)(2,1)}, u32[]{:S(2)}) copy-start(bf16[768]{0:T(1024)(128)(2,1)} %param.30) | copy-start | bytes 4612
  90.5 10.9 %copy-start.44 = (bf16[768]{0:T(1024)(128)(2,1)S(1)}, bf16[768]{0:T(1024)(128)(2,1)}, u32[]{:S(2)}) copy-start(bf16[768]{0:T(1024)(128)(2,1)} %param.28) | copy-start | bytes 4612
  90.5 10.9 %copy-start.45 = (bf16[768]{0:T(1024)(128)(2,1)S(1)}, bf16[768]{0:T(1024)(128)(2,1)}, u32[]{:S(2)}) copy-start(bf16[768]{0:T(1024)(128)(2,1)} %param.27) | copy-start | bytes 4612
  90.5 10.9 %copy-start.10 = (bf16[1,128,768]{2,1,0:T(8,128)(2,1)S(1)}, bf16[1,128,768]{2,1,0:T(8,128)(2,1)}, u32[]{:S(2)}) copy-start(bf16[1,128,768]{2,1,0:T(8,128)(2,1)} %param.17) | copy-start | bytes 589828
  90.5 10.9 %copy-start.36 = (f32[768]{0:T(1024)S(1)}, f32[768]{0:T(1024)}, u32[]{:S(2)}) copy-start(f32[768]{0:T(1024)} %convert_element_type.189) | copy-start | bytes 9220
  101.3 0.8 copy-start.39
  102.1 21.6 %copy-start.37 = (f32[128]{0:T(128)}, f32[128]{0:T(128)S(1)}, u32[]{:S(2)}) copy-start(f32[128]{0:T(128)S(1)} %broadcast_multiply_fusion.6) | copy-start | bytes 1540
  102.3 21.4 %copy-start.41 = (f32[128]{0:T(128)}, f32[128]{0:T(128)S(1)}, u32[]{:S(2)}) copy-start(f32[128]{0:T(128)S(1)} %add_rsqrt_fusion.2) | copy-start | bytes 1540
  113.5 10.3 %copy-start.47 = (bf16[768,768]{1,0:T(8,128)(2,1)S(1)}, bf16[768,768]{1,0:T(8,128)(2,1)}, u32[]{:S(2)}) copy-start(bf16[768,768]{1,0:T(8,128)(2,1)} %param.31) | copy-start | bytes 3538948
  123.7 3.6 copy-start.52
  125.5 1.9 copy-start.51
  129.2 317.6 %all-reduce.6.cloned.1.call-start = ((), (), s32[]{:S(2)}) async-start(), calls=%async_computation | async-start | bytes 589824 | tf_op jit(solution)/shard_map/psum | solution.py:478
  129.5 13.1 %copy-start.38 = (f32[128]{0:T(128)S(1)}, f32[128]{0:T(128)}, u32[]{:S(2)}) copy-start(f32[128]{0:T(128)} %copy-done.37) | copy-start | bytes 1540
  129.5 13.1 %copy-start.42 = (f32[128]{0:T(128)S(1)}, f32[128]{0:T(128)}, u32[]{:S(2)}) copy-start(f32[128]{0:T(128)} %copy-done.41) | copy-start | bytes 1540
  129.5 36.1 %slice-start = ((s8[12582912]{0:T(1024)(128)(4,1)}), s8[4194304]{0:T(1024)(128)(4,1)S(1)}, s32[]{:S(2)}) async-start(s8[12582912]{0:T(1024)(128)(4,1)} %bitcast.90), calls=%async_computation.2 | async-start | bytes 8388608
  131.6 11.3 %copy-start.33 = (f32[3,512]{1,0:T(4,128)S(1)}, f32[3,512]{1,0:T(4,128)}, u32[]{:S(2)}) copy-start(f32[3,512]{1,0:T(4,128)} %copy-done.32) | copy-start | bytes 18436
  131.6 11.3 %copy-start.27 = (bf16[1,128,768]{2,1,0:T(8,128)(2,1)S(1)}, bf16[1,128,768]{2,1,0:T(8,128)(2,1)}, u32[]{:S(2)}) copy-start(bf16[1,128,768]{2,1,0:T(8,128)(2,1)} %param.33) | copy-start | bytes 589828
  143.9 12.7 %copy-start.21 = (bf16[192,768]{1,0:T(8,128)(2,1)S(1)}, bf16[192,768]{1,0:T(8,128)(2,1)}, u32[]{:S(2)}) copy-start(bf16[192,768]{1,0:T(8,128)(2,1)} %param.25) | copy-start | bytes 884740
  144.1 21.5 %slice-start.1 = ((s8[12582912]{0:T(1024)(128)(4,1)}), s8[4194304]{0:T(1024)(128)(4,1)S(1)}, s32[]{:S(2)}) async-start(s8[12582912]{0:T(1024)(128)(4,1)} %bitcast.90), calls=%async_computation.3 | async-start | bytes 8388608
  156.6 0.9 copy-start.8
  157.5 8.0 %slice-start.2 = ((s8[12582912]{0:T(1024)(128)(4,1)}), s8[4194304]{0:T(1024)(128)(4,1)S(1)}, s32[]{:S(2)}) async-start(s8[12582912]{0:T(1024)(128)(4,1)} %bitcast.90), calls=%async_computation.4 | async-start | bytes 8388608
  170.2 4.7 %copy-start.25 = (bf16[512,192]{0,1:T(8,128)(2,1)S(1)}, bf16[512,192]{0,1:T(8,128)(2,1)}, u32[]{:S(2)}) copy-start(bf16[512,192]{0,1:T(8,128)(2,1)} %copy-done.24) | copy-start | bytes 589828
  174.9 5.1 %copy-start.5 = (bf16[3,512,2048]{2,1,0:T(8,128)(2,1)S(1)}, bf16[3,512,2048]{2,1,0:T(8,128)(2,1)}, u32[]{:S(2)}) copy-start(bf16[3,512,2048]{2,1,0:T(8,128)(2,1)} %multiply_convert_fusion) | copy-start | bytes 18874372
  174.9 5.1 %copy-start.7 = (bf16[2048,192]{0,1:T(8,128)(2,1)S(1)}, bf16[2048,192]{0,1:T(8,128)(2,1)}, u32[]{:S(2)}) copy-start(bf16[2048,192]{0,1:T(8,128)(2,1)} %copy-done.6) | copy-start | bytes 2359300
  180.0 2.7 copy-start.48
  180.0 2.7 copy-start.53
  182.7 1.7 copy-start.28
  193.4 104.4 %copy-start.23 = (bf16[768,192]{0,1:T(8,128)(2,1)S(1)}, bf16[768,192]{0,1:T(8,128)(2,1)}, u32[]{:S(2)}) copy-start(bf16[768,192]{0,1:T(8,128)(2,1)} %param.22) | copy-start | bytes 884740
  297.8 3.6 copy-start.12
  297.8 3.6 copy-start.15
  297.8 3.6 copy-start.29
  303.3 2.3 copy-start.13
  303.3 2.3 copy-start.31
  303.3 2.3 copy-start.35
  308.8 58.9 %copy-start.46 = (f32[128]{0:T(128)S(1)}, f32[128]{0:T(128)}, u32[]{:S(2)}) copy-start(f32[128]{0:T(128)} %get-tuple-element.106) | copy-start | bytes 1540
  308.8 58.9 %copy-start.40 = (f32[128]{0:T(128)S(1)}, f32[128]{0:T(128)}, u32[]{:S(2)}) copy-start(f32[128]{0:T(128)} %copy-done.39) | copy-start | bytes 1540
  314.4 1.2 copy-start.2
  315.6 1.1 copy-start.3
  367.6 2.9 copy-start.9
  372.9 2.3 copy-start.16
  375.2 2.1 copy-start.17
  377.4 1.3 copy-start.19
  378.7 1.7 copy-start.18
  378.7 69.9 %copy-start.1 = (bf16[768,768]{1,0:T(8,128)(2,1)S(1)}, bf16[768,768]{1,0:T(8,128)(2,1)}, u32[]{:S(2)}) copy-start(bf16[768,768]{1,0:T(8,128)(2,1)} %param.29) | copy-start | bytes 3538948
Sparse Core Ops, SparseCore 0:
  129.3 108.6 all-reduce.7
  373.1 73.7 all-reduce.5

commit v3 on v2

--- a/solution.py
+++ b/solution.py
@@ -262,10 +262,12 @@
     w,
     v_one,
     v_two,
+    early,
     term_out,
     mlp_out,
     w_out,
     v_out,
+    early_out,
     term_held,
     mlp_held,
     w_held,
@@ -312,6 +314,9 @@
         here = block(w_out, me, rows)
         return send(here, here, pairs[2], step - 1, far(step)[1])
 
+    def spread(step):
+        return send(early, block(early_out, me, early.shape[0]), pairs[6], step - 1, far(step)[1])
+
     def vector(step):
         return send(v_mine, v_held.at[step - 1], pairs[3], step - 1, far(step)[1])
 
@@ -325,6 +330,8 @@
     v_mine[0:8, :] = total
     v_mine[8:, :] = v_two[...]
     pl.loop(1, count)(lambda step: vector(step).start())
+    pl.loop(1, count)(lambda step: spread(step).start())
+    block(early_out, me, early.shape[0])[...] = early[...]
     w_total[...] = block(w, me, rows)[...].astype(f32)
 
     @pl.loop(1, count)
@@ -352,14 +359,20 @@
         first(step).wait_send()
         second(step).wait_send()
         vector(step).wait_send()
-
-
-def final(term, mlp, w, v_one, v_two, number):
+        spread(step).wait_recv()
+        spread(step).wait_send()
+
+
+def padded(w, count):
+    pad = -w.shape[0] % (16 * count)
+    return jnp.pad(w, ((0, pad), (0, 0))) if pad else w
+
+
+def final(term, mlp, w, v_one, v_two, early, number):
     n, dp, seq = lax.axis_size("tensor"), lax.axis_size("dp"), lax.axis_size("seq")
     f32, bf16 = jnp.float32, jnp.bfloat16
     count = dp * seq
-    pad = -w.shape[0] % (16 * count)
-    w = jnp.pad(w, ((0, pad), (0, 0))) if pad else w
+    w = padded(w, count)
     rows = term.shape[0] // n
     vectors = (8 + v_two.shape[0], 128)
     part = w.shape[0] // count
@@ -373,6 +386,7 @@
             jax.ShapeDtypeStruct((rows, term.shape[1]), f32),
             jax.ShapeDtypeStruct(w.shape, bf16),
             jax.ShapeDtypeStruct(vectors, f32),
+            jax.ShapeDtypeStruct((count * early.shape[0], early.shape[1]), bf16),
         ),
         [
             held,
@@ -385,13 +399,15 @@
         ]
         + near
         + far * 3
-        + near * 2,
+        + near * 2
+        + far,
         2**26,
         term,
         mlp,
         w,
         v_one,
         v_two,
+        early,
     )
 
 
@@ -472,10 +488,12 @@
     mlp_terms = product(hidden, w_down).astype(bf16)
     grad_down = product_rows(hidden, grad_z_all)
     grad_up = product_rows(mlp_input, grad_before)
-    grad_wout = product_rows(context, grad_attn_all)
-    early = lax.psum((grad_up.astype(bf16), grad_down.astype(bf16)), ("dp", "seq"))
-    grad_wout, early = lax.optimization_barrier((grad_wout.astype(bf16), early))
-    sum_wout = lax.psum(grad_wout, ("dp", "seq"))
+    early = padded(
+        jnp.concatenate([grad_up.astype(bf16), grad_down.astype(bf16)], axis=1),
+        lax.axis_size("dp") * lax.axis_size("seq"),
+    )
+    early = lax.psum_scatter(early, ("dp", "seq"), scatter_dimension=0, tiled=True)
+    grad_wout = product_rows(grad_attn_all, context)
     grad_context = (
         product_cols(grad_attn_all, w_out).astype(bf16).reshape(frames, heads, HEAD_DIM)
     )
@@ -515,12 +533,13 @@
         jnp.sum(grad_before.astype(f32), axis=0),
     ]
     ends = np.cumsum([part.shape[0] for part in mine])
-    grad_one, mlp_rows, late, totals = final(
+    grad_one, mlp_rows, late, totals, early = final(
         term.astype(bf16),
         mlp_terms,
-        grad_qkv.astype(bf16),
+        jnp.concatenate([grad_qkv.astype(bf16), grad_wout.astype(bf16)], axis=1),
         v_one,
         as_rows(jnp.concatenate(mine), 16),
+        early,
         8,
     )
     result = (middle + mlp_rows + b_down.astype(f32)).astype(bf16)
@@ -539,15 +558,15 @@
         late[:, :heads_width],
         bq,
         late[:, heads_width : 2 * heads_width],
-        late[:, 2 * heads_width :],
+        late[:, 2 * heads_width : 3 * heads_width],
         bv,
-        sum_wout.astype(f32),
+        late[:, 3 * heads_width :].T,
         bo,
         gain2,
         bias2,
-        early[0].astype(f32),
+        early[:width, : b_up.shape[0]].astype(f32),
         bu,
-        early[1].astype(f32),
+        early[:width, b_up.shape[0] :].astype(f32),
         bd,
     )
 

time: 456 us -> 424 us (0.930)
  waiting for transfers between devices: 64.9 us -> 0.04 us
  Pallas kernels: 254 us -> 282 us
  matrix products: 59.6 us -> 53.5 us
  other arithmetic: 28.5 us -> 33.3 us
  local copies, waits for them, and re-layouts: 33 us -> 37.6 us
    psum x2 -> x0, waiting for transfers between devices: 64.9 us -> none  [the longest x1 64.9 us: local(): sum_wout = lax.psum(grad_wout, ('dp', 'seq'))]
    pallas_call x8, Pallas kernels: 254 us -> 282 us  [call(): pl.pallas_call(kernel, out_shape=out_shape, in_specs=[vmem] * len(operand...]
    dot_general x1, matrix products: 8.02 us -> 3.3 us  [local(): jnp.einsum('hqk,qhd->khd', probs_low, grad_context, preferred_element_typ...]
    unnamed x119 -> x124, local copies, waits for them, and re-layouts: 10.1 us -> 13.1 us
  transfers between devices with their start and end apart: 2 -> 1, of which waited for: 1 -> 0; matrix products, arithmetic and copies ran while one was open for 15% -> 13% of each run, Pallas kernels for 39% -> 22%
where the time goes in v3:
time: 424 us; the launch traced here: 421 us
  Pallas kernels  282 us (67%)
  matrix products  53.5 us (13%)
  local copies, waits for them, and re-layouts  37.6 us (9%)
  other arithmetic  33.3 us (8%)
  between operations  15 us (4%)
    pallas_call x8, Pallas kernels, call(): pl.pallas_call(kernel, out_shape=out_shape, in_specs=[vmem] * len(operand...  282 us
    dot_general x6, matrix products, product(): return jnp.dot(left, right, preferred_element_type=jnp.float32)  17.2 us
    unnamed x124, local copies, waits for them, and re-layouts  13.1 us
  transfers between devices with their start and end apart: 1, of which 0 were waited for; matrix products, arithmetic and copies ran while one was open for 13% of the time, Pallas kernels for 22%

profile of v3, /device:TPU:0, one launch (start us, length us, event | category | flops | bytes accessed | tf_op | source)
XLA Modules:
  0.0 421.0 jit_solution(2643336138485928188)
XLA Ops:
  7.3 1.1 convert_reduce_fusion.4
  10.9 0.7 convert_element_type.188
  12.3 1.3 convert_element_type.186
  14.2 1.3 convert_element_type.191
  15.5 1.0 pad_maximum_fusion.3.x
  16.6 20.5 %shard_map.296 = bf16[512,1536]{1,0:T(8,128)(2,1)S(1)} custom-call(bf16[128,1536]{1,0:T(8,128)(2,1)S(1)} %pad_maximum_fusion.3.x), custom_call_target="tpu_custom_call" | custom-call | bytes 16777216 | tf_op jit(solution)/shard_map/pallas_call | solution.py:61
  37.2 1.0 convert_reduce_fusion.2
  38.9 1.1 convolution_convert_fusion.8
  40.0 1.8 copy.68
  41.7 1.4 fusion.25
  43.3 34.0 %shard_map.297 = bf16[2048,384]{1,0:T(8,128)(2,1)S(1)} custom-call(bf16[512,384]{1,0:T(8,128)(2,1)S(1)} %pad_maximum_fusion.4.x), custom_call_target="tpu_custom_call" | custom-call | bytes 33554432 | tf_op jit(solution)/shard_map/pallas_call | solution.py:61
  77.3 1.8 fusion.61
  79.1 1.4 copy.70
  80.6 2.5 copy.69
  83.1 1.6 fusion.26
  84.7 1.9 multiply_reduce_fusion.1
  86.7 2.5 fusion
  89.2 2.0 copy-done.9
  91.2 3.4 fusion.28
  95.1 10.3 %shard_map.298 = f32[128,768]{1,0:T(8,128)S(1)} custom-call(bf16[512,768]{1,0:T(8,128)(2,1)S(1)} %convolution_convert_fusion.5.x), custom_call_target="tpu_custom_call" | custom-call | bytes 16777216 | tf_op jit(solution)/shard_map/pallas_call | solution.py:61
  105.4 0.7 fusion.59
  106.5 11.0 %shard_map.299 = bf16[512,768]{1,0:T(8,128)(2,1)S(1)} custom-call(bf16[128,768]{1,0:T(8,128)(2,1)S(1)} %add_convert_fusion.2.x), custom_call_target="tpu_custom_call" | custom-call | bytes 16777216 | tf_op jit(solution)/shard_map/pallas_call | solution.py:61
  117.6 10.4 %multiply_convert_fusion.1 = (bf16[512,768]{1,0:T(8,128)(2,1)S(1)}, f32[512,768]{1,0:T(8,128)S(1)}, f32[512,768]{1,0:T(8,128)S(1)}) fusion(f32[768]{0:T(1024)S(1)} %copy-done.46, bf16[512,768]{1,0:T(8,128)(2,1)S(1)} %shard_map.299, bf16[768,768]{1,0:T(8,128)(2,1)S(1)} %copy-done), kind=kOutput, calls=%fused_computation.32 | convolution fusion | flops 629932032 | bytes 5901312 | tf_op jit(solution)/shard_map/dot_general | solution.py:18
  128.0 1.7 convert_reduce_fusion.1
  129.7 0.8 convolution_convert_fusion.1
  130.6 0.8 convolution_convert_fusion
  131.4 1.6 pad_maximum_fusion
  133.1 1.9 convolution_convert_fusion.4.x
  135.0 11.0 %shard_map.300 = f32[128,768]{1,0:T(8,128)S(1)} custom-call(bf16[512,768]{1,0:T(8,128)(2,1)S(1)} %convolution_convert_fusion.4.x), custom_call_target="tpu_custom_call" | custom-call | bytes 16777216 | tf_op jit(solution)/shard_map/pallas_call | solution.py:61
  146.4 0.9 fusion.58
  147.5 12.1 %shard_map.301 = bf16[576,768]{1,0:T(8,128)(2,1)S(1)} custom-call(bf16[144,768]{1,0:T(8,128)(2,1)S(1)} %maximum_maximum_fusion.x), custom_call_target="tpu_custom_call" | custom-call | bytes 16777216 | tf_op jit(solution)/shard_map/pallas_call | solution.py:61
  159.8 1.0 convolution_convert_fusion.6
  161.3 1.3 dynamic_slice.11
  163.2 1.9 copy.75
  165.1 6.7 %multiply_reduce_fusion = (f32[3,512]{1,0:T(4,128)S(1)}, f32[3,512,2048]{2,1,0:T(8,128)S(1)}) fusion(f32[3,512,2048]{2,1,0:T(8,128)} %copy-done.9, f32[3,512]{1,0:T(4,128)S(1)} %log_add_fusion, bf16[512,3,64]{0,2,1:T(8,128)(2,1)S(1)} %bitcast.103, bf16[2048,3,64]{0,2,1:T(8,128)(2,1)S(1)} %bitcast.100), kind=kOutput, calls=%fused_computation.1 | convolution fusion | flops 415234560 | bytes 26161152 | tf_op jit(solution)/shard_map/qhd,khd->hqk/dot_general | solution.py:503
  172.3 1.2 slice-done.2
  173.6 4.7 %multiply_convert_fusion = bf16[3,512,2048]{2,1,0:T(8,128)(2,1)} fusion(f32[3,512,2048]{2,1,0:T(8,128)S(1)} %get-tuple-element.119, f32[3,512,2048]{2,1,0:T(8,128)S(1)} %bitcast.93, f32[3,512]{1,0:T(4,128)S(1)} %get-tuple-element.118, f32[3,512]{1,0:T(4,128)S(1)} %log_add_fusion), kind=kLoop, calls=%fused_computation | loop fusion | flops 15728640 | bytes 31469568 | tf_op jit(solution)/shard_map/convert_element_type | solution.py:505
  178.2 3.3 fusion.8
  181.5 2.3 copy.72
  183.8 4.9 %convert_reduce_fusion.6 = (f32[3,64]{1,0:T(4,128)S(1)}, bf16[3,64,512]{2,1,0:T(8,128)(2,1)S(1)}) fusion(bf16[2048,3,64]{0,2,1:T(8,128)(2,1)S(1)} %bitcast.95, bf16[3,512,2048]{2,1,0:T(8,128)(2,1)} %multiply_convert_fusion), kind=kOutput, calls=%fused_computation.93 | convolution fusion | flops 403046208 | bytes 7275264 | tf_op jit(solution)/shard_map/hqk,khd->qhd/dot_general | solution.py:513
  189.4 0.8 copy.73
  190.2 4.1 fusion.7
  194.3 1.3 copy.71
  195.6 2.2 pad_maximum_fusion.1.x
  197.8 71.7 %shard_map.302 = f32[512,384]{1,0:T(8,128)S(1)} custom-call(bf16[2048,384]{1,0:T(8,128)(2,1)S(1)} %pad_maximum_fusion.1.x), custom_call_target="tpu_custom_call" | custom-call | bytes 33554432 | tf_op jit(solution)/shard_map/pallas_call | solution.py:61
  269.6 1.8 convolution_convert_fusion.2
  271.4 2.3 copy.74
  273.7 1.4 fusion.67
  276.0 1.7 fusion.17
  278.1 1.1 convert_reduce_fusion.5
  279.2 0.8 concatenate.32
  280.1 1.5 pad_maximum_fusion.2.w
  282.1 2.3 convolution_convert_fusion.3.mlp
  284.5 1.0 copy-done.8
  285.4 111.1 %shard_map.303 = (f32[128,768]{1,0:T(8,128)S(1)}, f32[128,768]{1,0:T(8,128)S(1)}, bf16[768,768]{1,0:T(8,128)(2,1)S(1)}, f32[24,128]{1,0:T(8,128)S(1)}, bf16[768,1536]{1,0:T(8,128)(2,1)S(1)}) custom-call(bf16[512,768]{1,0:T(8,128)(2,1)S(1)} %get-tuple-element.96.term, bf16[512,768]{1,0:T(8,128)(2,1)S(1)} %convolution_convert_fusion.3.mlp, ...), custom_call_target="tpu_custom_call" | custom-call | bytes 67108864 | tf_op jit(solution)/shard_map/pallas_call | solution.py:61
  398.0 1.4 fusion.62
  402.1 1.2 slice_bitcast_fusion
  403.2 2.2 copy.81
  405.4 1.1 copy.80
  406.5 2.3 copy.79
  408.9 1.1 copy.78
  410.0 2.5 slice_convert_fusion
  412.5 0.7 fusion.51
  413.3 0.9 fusion.52
  (175 shorter events, 14.7 us)
Async XLA Ops:
  7.2 110.3 %copy-start = (bf16[768,768]{1,0:T(8,128)(2,1)S(1)}, bf16[768,768]{1,0:T(8,128)(2,1)}, u32[]{:S(2)}) copy-start(bf16[768,768]{1,0:T(8,128)(2,1)} %param.29) | copy-start | bytes 3538948
  7.2 277.2 %reduce-scatter.2.cloned.1.call-start = ((), (), s32[]{:S(2)}) async-start(), calls=%async_computation.1 | async-start | bytes 2654208 | tf_op jit(solution)/shard_map/reduce_scatter | solution.py:495
  10.9 27.4 %copy-start.35 = (f32[768]{0:T(1024)}, f32[768]{0:T(1024)S(1)}, u32[]{:S(2)}) copy-start(f32[768]{0:T(1024)S(1)} %convert_element_type.173) | copy-start | bytes 9220
  11.6 94.8 %copy-start.37 = (f32[768]{0:T(1024)}, f32[768]{0:T(1024)S(1)}, u32[]{:S(2)}) copy-start(f32[768]{0:T(1024)S(1)} %convert_element_type.188) | copy-start | bytes 9220
  37.2 1.4 copy-start.39
  37.2 1.6 copy-start.26
  38.3 0.6 copy-start.41
  38.9 4.3 %copy-start.20 = (bf16[512,768]{1,0:T(8,128)(2,1)}, bf16[512,768]{1,0:T(8,128)(2,1)S(1)}, u32[]{:S(2)}) copy-start(bf16[512,768]{1,0:T(8,128)(2,1)S(1)} %fusion.16) | copy-start | bytes 2359300
  41.7 1.4 copy-start.29
  80.5 4.2 copy-start.12
  84.7 2.0 copy-start.28
  86.7 4.5 %copy-start.9 = (f32[3,512,2048]{2,1,0:T(8,128)}, f32[3,512,2048]{2,1,0:T(8,128)S(1)}, u32[]{:S(2)}) copy-start(f32[3,512,2048]{2,1,0:T(8,128)S(1)} %get-tuple-element.116) | copy-start | bytes 37748740
  86.7 4.5 %copy-start.17 = (bf16[2048,192]{0,1:T(8,128)(2,1)S(1)}, bf16[2048,192]{0,1:T(8,128)(2,1)}, u32[]{:S(2)}) copy-start(bf16[2048,192]{0,1:T(8,128)(2,1)} %copy.69) | copy-start | bytes 2359300
  91.2 3.4 copy-start.24
  94.6 11.6 %copy-start.30 = (bf16[3,64,512]{2,1,0:T(8,128)(2,1)}, bf16[3,64,512]{2,1,0:T(8,128)(2,1)S(1)}, u32[]{:S(2)}) copy-start(bf16[3,64,512]{2,1,0:T(8,128)(2,1)S(1)} %fusion.28) | copy-start | bytes 589828
  94.6 10.8 %copy-start.14 = (bf16[1,128,768]{2,1,0:T(8,128)(2,1)S(1)}, bf16[1,128,768]{2,1,0:T(8,128)(2,1)}, u32[]{:S(2)}) copy-start(bf16[1,128,768]{2,1,0:T(8,128)(2,1)} %param.17) | copy-start | bytes 589828
  94.6 10.8 %copy-start.43 = (f32[768]{0:T(1024)S(1)}, f32[768]{0:T(1024)}, u32[]{:S(2)}) copy-start(f32[768]{0:T(1024)} %convert_element_type.186) | copy-start | bytes 9220
  94.6 10.8 %copy-start.44 = (f32[128]{0:T(128)S(1)}, f32[128]{0:T(128)}, u32[]{:S(2)}) copy-start(f32[128]{0:T(128)} %broadcast_multiply_fusion.3) | copy-start | bytes 1540
  105.4 12.1 %copy-start.46 = (f32[768]{0:T(1024)S(1)}, f32[768]{0:T(1024)}, u32[]{:S(2)}) copy-start(f32[768]{0:T(1024)} %convert_element_type.191) | copy-start | bytes 9220
  106.1 40.3 %copy-start.10 = (f32[128,768]{1,0:T(8,128)}, f32[128,768]{1,0:T(8,128)S(1)}, u32[]{:S(2)}) copy-start(f32[128,768]{1,0:T(8,128)S(1)} %get-tuple-element.93) | copy-start | bytes 1179652
  117.5 10.4 %copy-start.53 = (bf16[768,768]{1,0:T(8,128)(2,1)S(1)}, bf16[768,768]{1,0:T(8,128)(2,1)}, u32[]{:S(2)}) copy-start(bf16[768,768]{1,0:T(8,128)(2,1)} %param.31) | copy-start | bytes 3538948
  128.0 2.6 copy-start.55
  129.7 0.9 copy-start.54
  133.0 13.0 %copy-start.38 = (f32[768]{0:T(1024)S(1)}, f32[768]{0:T(1024)}, u32[]{:S(2)}) copy-start(f32[768]{0:T(1024)} %copy-done.37) | copy-start | bytes 9220
  135.0 11.4 %copy-start.32 = (bf16[1,128,768]{2,1,0:T(8,128)(2,1)S(1)}, bf16[1,128,768]{2,1,0:T(8,128)(2,1)}, u32[]{:S(2)}) copy-start(bf16[1,128,768]{2,1,0:T(8,128)(2,1)} %param.33) | copy-start | bytes 589828
  147.5 12.3 %copy-start.31 = (bf16[3,64,512]{2,1,0:T(8,128)(2,1)S(1)}, bf16[3,64,512]{2,1,0:T(8,128)(2,1)}, u32[]{:S(2)}) copy-start(bf16[3,64,512]{2,1,0:T(8,128)(2,1)} %copy-done.30) | copy-start | bytes 589828
  159.7 1.1 copy-start.25
  159.8 1.5 copy-start.49
  159.8 5.3 %copy-start.18 = (bf16[2048,192]{0,1:T(8,128)(2,1)S(1)}, bf16[2048,192]{0,1:T(8,128)(2,1)}, u32[]{:S(2)}) copy-start(bf16[2048,192]{0,1:T(8,128)(2,1)} %copy.69) | copy-start | bytes 2359300
  165.1 6.8 %slice-start = ((s8[12582912]{0:T(1024)(128)(4,1)}), s8[4194304]{0:T(1024)(128)(4,1)S(1)}, s32[]{:S(2)}) async-start(s8[12582912]{0:T(1024)(128)(4,1)} %bitcast.92), calls=%async_computation.2 | async-start | bytes 8388608
  165.1 7.2 %slice-start.1 = ((s8[12582912]{0:T(1024)(128)(4,1)}), s8[4194304]{0:T(1024)(128)(4,1)S(1)}, s32[]{:S(2)}) async-start(s8[12582912]{0:T(1024)(128)(4,1)} %bitcast.92), calls=%async_computation.3 | async-start | bytes 8388608
  165.1 8.4 %slice-start.2 = ((s8[12582912]{0:T(1024)(128)(4,1)}), s8[4194304]{0:T(1024)(128)(4,1)S(1)}, s32[]{:S(2)}) async-start(s8[12582912]{0:T(1024)(128)(4,1)} %bitcast.92), calls=%async_computation.4 | async-start | bytes 8388608
  181.5 2.3 copy-start.13
  197.8 71.7 %copy-start.21 = (bf16[512,768]{1,0:T(8,128)(2,1)S(1)}, bf16[512,768]{1,0:T(8,128)(2,1)}, u32[]{:S(2)}) copy-start(bf16[512,768]{1,0:T(8,128)(2,1)} %copy-done.20) | copy-start | bytes 2359300
  197.8 71.7 %copy-start.34 = (bf16[512,192]{1,0:T(8,128)(2,1)S(1)}, bf16[512,192]{1,0:T(8,128)(2,1)}, u32[]{:S(2)}) copy-start(bf16[512,192]{1,0:T(8,128)(2,1)} %copy.73) | copy-start | bytes 589828
  269.5 5.5 %copy-start.19 = (bf16[512,384]{1,0:T(8,128)(2,1)}, bf16[512,384]{1,0:T(8,128)(2,1)S(1)}, u32[]{:S(2)}) copy-start(bf16[512,384]{1,0:T(8,128)(2,1)S(1)} %convert_element_type.204) | copy-start | bytes 1179652
  271.4 3.6 copy-start.27
  275.0 1.0 copy-start.33
  275.1 1.0 copy-start.40
  275.1 0.9 copy-start.42
  277.7 3.9 copy-start.50
  284.4 1.0 copy-start.8
  396.5 1.4 copy-start.2
  396.5 1.5 copy-start.6
  396.5 2.9 copy-start.4
  398.0 1.4 copy-start.15
  398.0 1.4 copy-start.36
  398.0 1.4 copy-start.45
  398.0 1.4 copy-start.47
  405.4 3.4 copy-start.22
  406.5 3.4 copy-start.3
  409.9 2.6 copy-start.7
  409.9 2.6 copy-start.11
  409.9 3.3 copy-start.5
  409.9 3.3 copy-start.16
  410.0 3.3 copy-start.23
  410.0 3.3 copy-start.48
  410.0 3.3 copy-start.51
  410.0 3.3 copy-start.52
  410.0 4.2 copy-start.1
Sparse Core Ops, SparseCore 0:
  133.1 69.3 reduce-scatter.1
